TPU v7x, 128 devices: a whole 4x4x4 slice. The times are simulated.
128 devices in a mesh: dp: 8 (over x, core), seq: 8 (over z_hi, y), tensor: 2 (over z_lo).
Axes of the slice: x: 4, y: 4, z: 4 (z_hi: 2, z_lo: 2; z = z_hi * 2 + z_lo), core: 2. Of those that a mesh axis runs over, the one named last changes fastest.
Arguments:
- hidden_in: bfloat16 [8, 1024, 2048], P('dp', 'seq'), may hold values from -6 to 6
- grad_out: bfloat16 [8, 1024, 2048], P('dp', 'seq'), may hold values from -6 to 6
- expert_ids: int32 [8, 1024, 4], P('dp', 'seq'), may hold values from 0 to 7, all different within a row
- slot_rank: int32 [8, 1024, 4], P('dp', 'seq'), may hold values from 0 to 511, as said below
- piece_start: int32 [8, 2], P('dp'), may hold values from 0 to 768, as said below
- norm_attn: bfloat16 [2048], P(('dp', 'seq')), may hold values from 0.5 to 1.5
- w_qkv: bfloat16 [2048, 3, 2048], P(('dp', 'seq'), None, 'tensor'), may hold values from -0.125 to 0.125
- b_qkv: bfloat16 [3, 16, 128], P(None, 'tensor', ('dp', 'seq')), may hold values from -1.796875 to 1.796875
- w_proj: bfloat16 [2048, 2048], P('tensor', ('dp', 'seq')), may hold values from -1 to 1
- norm_ffn: bfloat16 [2048], P(('dp', 'seq')), may hold values from 0.5 to 1.5
- w_router: bfloat16 [2048, 8], P(('dp', 'seq')), may hold values from -0.0625 to 0.0625
- w_share_gate: bfloat16 [2048], P(('dp', 'seq')), may hold values from -0.125 to 0.125
- expert_gate_up: bfloat16 [2048, 8, 2, 1408], P(('dp', 'seq'), None, None, 'tensor'), may hold values from -0.125 to 0.125
- expert_down: bfloat16 [8, 1408, 2048], P(None, 'tensor', ('dp', 'seq')), may hold values from -0.4375 to 0.4375
- shared_gate_up: bfloat16 [2048, 2, 5632], P(('dp', 'seq'), None, 'tensor'), may hold values from -0.125 to 0.125
- shared_down: bfloat16 [5632, 2048], P('tensor', ('dp', 'seq')), may hold values from -0.15625 to 0.15625
Outputs:
- hidden_out: bfloat16 [8, 1024, 2048], P('dp', 'seq')
- grad_in: float32 [8, 1024, 2048], P('dp', 'seq')
- grad_norm_attn: float32 [2048], P(('dp', 'seq'))
- grad_w_qkv: float32 [2048, 3, 2048], P(('dp', 'seq'), None, 'tensor')
- grad_b_qkv: float32 [3, 16, 128], P(None, 'tensor', ('dp', 'seq'))
- projection_weight_gradient: float32 [2048, 2048], P('tensor', ('dp', 'seq'))
- grad_norm_ffn: float32 [2048], P(('dp', 'seq'))
- grad_w_router: float32 [2048, 8], P(('dp', 'seq'))
- grad_share_gate: float32 [2048], P(('dp', 'seq'))
- grad_expert_gate_up: float32 [2048, 8, 2, 1408], P(('dp', 'seq'), None, None, 'tensor')
- expert_down_gradient: float32 [8, 1408, 2048], P(None, 'tensor', ('dp', 'seq'))
- grad_shared_gate_up: float32 [2048, 2, 5632], P(('dp', 'seq'), None, 'tensor')
- grad_shared_down: float32 [5632, 2048], P('tensor', ('dp', 'seq'))
Inputs may be any that keep to these rules, and one draw needn't show every extreme that they name: `expert_ids`: each token names 4 different experts. `slot_rank`: in every aligned block of 128 tokens of a sequence, the 512 entries take each value once. `piece_start`: the 2 picture pieces of a sequence, 256 tokens each, lie in increasing order, apart from each other and inside the sequence.
All inputs are finite; a program needn't handle non-finite values.
Results may differ from a plain program's by a relative error of at most 0.025.
Values may be sent and summed in bfloat16 or wider, within the bound.
No kernel may reach another device: no remote copies, remote signals or barrier semaphores. Data moves between devices by JAX's collectives and lax.ppermute only.
A program may use at most 576 MiB of HBM per device.

v0:
```python
import math

import jax
import jax.numpy as jnp
from jax import lax
from jax.experimental import pallas as pl
from jax.experimental.pallas import tpu as pltpu
from jax.sharding import Mesh
from jax.sharding import PartitionSpec as P

HD = 128
TOPK = 4
PIC = 256

EPS = 1e-06
THETA = 1000000.0
MASKED = -1000000000.0

SEQ = ("z_hi", "ring")
GRID = ("z_hi", "ring", "tensor")
BF = jnp.bfloat16
F32 = jnp.float32
LANES = 128


def up_to(size, multiple):
    return -(-size // multiple) * multiple


def dot(a, b, dims):
    return lax.dot_general(a, b, (dims, ((), ())), preferred_element_type=F32)


def mm(a, b):
    return dot(a, b, ((1,), (0,)))


def mm_nt(a, b):
    return dot(a, b, ((1,), (1,)))


def mm_tn(a, b):
    return dot(a, b, ((0,), (0,)))


def rms_scale(values):
    return lax.rsqrt(jnp.mean(values * values, axis=-1, keepdims=True) + EPS)


def silu_grads(act_grad, gate_val, up_val):
    gate_sigmoid = jax.nn.sigmoid(gate_val)
    gate_grad = act_grad * up_val * gate_sigmoid * (1.0 + gate_val * (1.0 - gate_sigmoid))
    up_grad = act_grad * (gate_val * gate_sigmoid)
    return (gate_grad, up_grad)


def from_facing(x):
    flip = lax.axis_size("ring") * 2 + 1
    count = 2 * lax.axis_size("ring") * 2
    return lax.ppermute(x, GRID, [(i, i ^ flip) for i in range(count)])


def swap(x):
    return lax.ppermute(x, "tensor", [(0, 1), (1, 0)])


def together(*arrays):
    return lax.optimization_barrier(arrays)


UNITS = 384
VMEM = 56 * 1024 * 1024


def feed_forward_kernel(h_ref, dy_ref, up_ref, down_ref, scale_ref, middle_ref, act_ref, dot_ref):
    routed = pl.program_id(0) < pl.num_programs(0) - 1
    tokens = h_ref.shape[0]
    step = 256

    @pl.when(pl.program_id(0) == 0)
    def _():
        dot_ref[...] = jnp.zeros_like(dot_ref)

    for at in range(0, tokens, step):
        here = pl.ds(at, step)
        gate_up = mm(h_ref[here, :], up_ref[...])
        back = mm(dy_ref[here, :], down_ref[...])
        gate, up = gate_up[:, :UNITS], gate_up[:, UNITS:]
        scale = jnp.where(routed, scale_ref[here, 0:1], scale_ref[here, 1:2])
        sigma = jax.nn.sigmoid(gate)
        silu = gate * sigma
        act = (silu * up).astype(BF).astype(F32)
        dots = jnp.sum(act * back, axis=1, keepdims=True)
        place = lax.broadcasted_iota(jnp.int32, (step, LANES), 1)
        place = place == jnp.where(routed, 0, 1)
        dot_ref[here, :] += jnp.where(place, dots, 0.0)
        back = back * scale
        act_ref[here, :] = (act * scale).astype(BF)
        middle_ref[here, :UNITS] = (back * up * sigma * (1.0 + gate * (1.0 - sigma))).astype(BF)
        middle_ref[here, UNITS:] = (back * silu).astype(BF)


def feed_forward(h, dy, weights, scales):
    tokens, width = h.shape
    parts = weights.shape[1] // (3 * UNITS)

    def whole(columns):
        return pl.BlockSpec((tokens, columns), lambda i: (0, 0), pipeline_mode=pl.Buffered(1))

    return pl.pallas_call(
        feed_forward_kernel,
        grid=(parts,),
        in_specs=[
            whole(width),
            whole(width),
            pl.BlockSpec((width, 2 * UNITS), lambda i: (0, i)),
            pl.BlockSpec((width, UNITS), lambda i: (0, 2 * parts + i)),
            whole(LANES),
        ],
        out_specs=[
            pl.BlockSpec((tokens, 2 * UNITS), lambda i: (0, i)),
            pl.BlockSpec((tokens, UNITS), lambda i: (0, i)),
            pl.BlockSpec((tokens, LANES), lambda i: (0, 0)),
        ],
        out_shape=[
            jax.ShapeDtypeStruct((tokens, 2 * UNITS * parts), BF),
            jax.ShapeDtypeStruct((tokens, UNITS * parts), BF),
            jax.ShapeDtypeStruct((tokens, LANES), F32),
        ],
        compiler_params=pltpu.CompilerParams(vmem_limit_bytes=VMEM),
    )(h, dy, weights, weights, scales)


def ffn_grads_kernel(h_ref, dy_ref, middle_ref, act_ref, grad_ref):
    ups = middle_ref.shape[1]
    grad_ref[:, :ups] = mm_tn(h_ref[...], middle_ref[...]).astype(BF)
    grad_ref[:, ups:] = mm_tn(dy_ref[...], act_ref[...]).astype(BF)


def ffn_grads(h, dy, middle, act):
    tokens, width = h.shape
    ups, downs = middle.shape[1], act.shape[1]
    step = 256
    return pl.pallas_call(
        ffn_grads_kernel,
        grid=(width // step,),
        in_specs=[
            pl.BlockSpec((tokens, step), lambda i: (0, i)),
            pl.BlockSpec((tokens, step), lambda i: (0, i)),
            pl.BlockSpec((tokens, ups), lambda i: (0, 0)),
            pl.BlockSpec((tokens, downs), lambda i: (0, 0)),
        ],
        out_specs=pl.BlockSpec((step, ups + downs), lambda i: (i, 0)),
        out_shape=jax.ShapeDtypeStruct((width, ups + downs), BF),
        compiler_params=pltpu.CompilerParams(vmem_limit_bytes=VMEM),
    )(h, dy, middle, act)


def attn_grads_kernel(h_ref, linear_ref, small_ref, dx_ref, heads_ref, grad_ref):
    qkv = linear_ref.shape[1]
    grad_ref[:, :qkv] = mm_tn(h_ref[...], linear_ref[...]).astype(BF)
    grad_ref[:, qkv : qkv + LANES] = small_ref[...].T.astype(BF)
    grad_ref[:, qkv + LANES :] = mm_tn(dx_ref[...], heads_ref[...]).astype(BF)


def attn_grads(h, linear, small, dx, heads):
    tokens, width = h.shape
    rows, heads_width = heads.shape
    qkv = linear.shape[1]
    columns = qkv + LANES + heads_width
    step = 256
    return pl.pallas_call(
        attn_grads_kernel,
        grid=(width // step,),
        in_specs=[
            pl.BlockSpec((tokens, step), lambda i: (0, i)),
            pl.BlockSpec((tokens, qkv), lambda i: (0, 0)),
            pl.BlockSpec((LANES, step), lambda i: (0, i)),
            pl.BlockSpec((rows, step), lambda i: (0, i)),
            pl.BlockSpec((rows, heads_width), lambda i: (0, 0)),
        ],
        out_specs=pl.BlockSpec((step, columns), lambda i: (i, 0)),
        out_shape=jax.ShapeDtypeStruct((width, columns), BF),
        compiler_params=pltpu.CompilerParams(vmem_limit_bytes=VMEM),
    )(h, linear, small, dx, heads)


def plane_gather(x):
    n, width = x.shape
    count = lax.axis_size(SEQ) * lax.axis_size("tensor")
    copies = jnp.broadcast_to(x[None], (count, n, width))
    return lax.all_to_all(copies, GRID, 0, 0, tiled=True).reshape(count * n, width)


def send_parts(parts):
    count = lax.axis_size(SEQ) * lax.axis_size("tensor")
    parts = parts.astype(BF).reshape(count, -1, parts.shape[-1])
    return lax.all_to_all(parts, GRID, 0, 0, tiled=True)


def sum_parts(parts):
    return jnp.sum(parts.astype(F32), axis=0)


def plane_scatter(parts):
    return sum_parts(send_parts(parts))


def body(
    hidden_in,
    grad_out,
    expert_ids,
    slot_rank,
    piece_start,
    norm_attn,
    w_qkv,
    b_qkv,
    w_proj,
    norm_ffn,
    w_router,
    w_share_gate,
    expert_gate_up,
    expert_down,
    shared_gate_up,
    shared_down,
):
    seqs = lax.axis_size(SEQ)
    dps = lax.axis_size("dp")
    me_seq = lax.axis_index(SEQ)
    me_tensor = lax.axis_index("tensor")
    me = me_seq * 2 + me_tensor
    rows = hidden_in.shape[1]
    own = rows // 2
    length = rows * seqs
    depth = w_qkv.shape[0]
    width = depth * dps * seqs
    experts = expert_gate_up.shape[1]
    fe = expert_gate_up.shape[3]
    fs = shared_gate_up.shape[2] // seqs
    fe_pad = up_to(fe, UNITS)
    fs_pad = up_to(fs, UNITS)
    bias_part = b_qkv.shape[2]
    heads = b_qkv.shape[1]
    capacity = (5 * rows * TOPK + 4 * experts - 1) // (4 * experts)
    score_scale = 1.0 / math.sqrt(HD)

    def mine(x):
        return lax.dynamic_slice_in_dim(x, me_tensor * own, own, 0)

    def both_halves(x):
        other = swap(x)
        first = jnp.where(me_tensor == 0, x, other)
        second = jnp.where(me_tensor == 0, other, x)
        return jnp.concatenate([first, second], 0)

    flat_ids = expert_ids[0].reshape(-1)
    flat_rank = slot_rank[0].reshape(-1)
    earlier = (flat_rank[None, :] < flat_rank[:, None]) & (flat_ids[None, :] == flat_ids[:, None])
    position = jnp.sum(earlier.astype(jnp.int32), axis=1)
    position = jnp.where(position < capacity, position, LANES - 1)
    chosen = expert_ids[0][:, :, None] == jnp.arange(experts, dtype=jnp.int32)[None, None, :]
    slot_of = jnp.sum(
        jnp.where(chosen, position.reshape(rows, TOPK)[:, :, None] - (LANES - 1), 0), axis=1
    ) + (LANES - 1)
    slot_cols = jnp.pad(slot_of.astype(BF), ((0, 0), (0, LANES - experts)))
    dy_own = mine(grad_out[0])
    dy_slots = jnp.concatenate([grad_out[0], slot_cols], 1)
    x_own = mine(hidden_in[0])

    misc = jnp.concatenate(
        [norm_attn[:, None], norm_ffn[:, None], w_share_gate[:, None], w_router], axis=1
    )
    n_misc = misc.shape[1]
    bias_rows = b_qkv.transpose(1, 0, 2).reshape(heads, 3 * bias_part)
    bias_rows = jnp.pad(bias_rows, ((0, 0), (0, depth - 3 * bias_part)))
    attn_blob = jnp.concatenate(
        [
            w_qkv.reshape(depth, 3, heads, HD).transpose(2, 0, 1, 3).reshape(heads, depth, 3 * HD),
            jnp.broadcast_to(misc[None], (heads, depth, n_misc)),
            bias_rows[:, :, None],
            jnp.zeros((heads, depth, LANES - n_misc - 1), BF),
        ],
        axis=2,
    )
    def padded(x, units):
        return jnp.pad(x, ((0, 0), (0, 0), (0, units - x.shape[2])))

    units = fe_pad + fs_pad
    egu_blob = expert_gate_up.transpose(1, 2, 0, 3)
    sgu_blob = shared_gate_up.reshape(depth, 2, seqs, fs).transpose(2, 1, 0, 3)
    edn_blob = expert_down.transpose(0, 2, 1)
    sdn_blob = shared_down.reshape(seqs, fs, depth).transpose(0, 2, 1)
    columns = []
    for blob, blob_units in ((egu_blob, fe_pad), (sgu_blob, fs_pad)):
        gates, ups = padded(blob[:, 0], blob_units), padded(blob[:, 1], blob_units)
        for at in range(0, blob_units, UNITS):
            columns += [gates[:, :, at : at + UNITS], ups[:, :, at : at + UNITS]]
    columns += [padded(edn_blob, fe_pad), padded(sdn_blob, fs_pad)]
    ffn_blob = jnp.concatenate(columns, axis=2)

    facing = from_facing(dy_slots)
    first_ring = lax.axis_index("z_hi") == 0
    dy_slots = jnp.stack(
        [jnp.where(first_ring, dy_slots, facing), jnp.where(first_ring, facing, dy_slots)]
    )

    x_all = plane_gather(x_own)
    proj_rows = lax.all_gather(w_proj.T, ("dp", *SEQ), axis=0, tiled=True)

    x_all, attn_blob = together(x_all, attn_blob)
    attn_blob = lax.all_to_all(attn_blob, SEQ, 0, 0, tiled=True).reshape(1, seqs * depth, -1)
    attn_full = jnp.broadcast_to(attn_blob, (dps, *attn_blob.shape[1:]))
    attn_full = lax.all_to_all(attn_full, "dp", 0, 0, tiled=True).reshape(width, -1)
    qkv_full = attn_full[:, : 3 * HD]
    misc_full = attn_full[:, 3 * HD :]

    attn_full, ffn_blob, dy_slots, proj_rows = together(attn_full, ffn_blob, dy_slots, proj_rows)
    dy_slots = lax.all_gather(dy_slots, "ring", axis=1, tiled=True)
    ffn_blob = lax.all_to_all(ffn_blob, SEQ, 0, 0, tiled=True)

    bias_full = misc_full[:, n_misc].reshape(dps * seqs, depth)[:, : 3 * bias_part]
    bias_full = bias_full.reshape(dps * seqs, 3, bias_part).transpose(1, 0, 2).reshape(1, 3 * HD)
    misc_rows = misc_full[:, :n_misc].T.astype(F32)
    gain_attn = misc_rows[0:1]
    gain_ffn = misc_rows[1:2]

    positions = jnp.arange(length, dtype=jnp.int32)
    freq_table = jnp.exp(jnp.arange(HD // 2, dtype=F32) * (-2.0 * math.log(THETA) / HD))
    angle = positions.astype(F32)[:, None] * freq_table[None, :]
    cosine = jnp.cos(angle)
    sine = jnp.sin(angle)
    starts = piece_start[0]
    inside = (positions[:, None] >= starts[None, :]) & (
        positions[:, None] < starts[None, :] + PIC
    )
    labels = jnp.arange(starts.shape[0], dtype=jnp.int32)
    segment = jnp.max(jnp.where(inside, labels[None, :], -1), axis=1)

    def seen():
        causal = positions[None, :] <= positions[:, None]
        picture = (segment[:, None] == segment[None, :]) & (segment[:, None] >= 0)
        return causal | picture

    def rotate(values):
        lead, tail = values[:, : HD // 2], values[:, HD // 2 :]
        return jnp.concatenate([lead * cosine - tail * sine, tail * cosine + lead * sine], axis=1)

    def unrotate(values):
        lead, tail = values[:, : HD // 2], values[:, HD // 2 :]
        return jnp.concatenate([lead * cosine + tail * sine, tail * cosine - lead * sine], axis=1)

    resid_all = x_all.astype(F32)
    norm_one = resid_all * rms_scale(resid_all)
    normed_one = (norm_one * gain_attn).astype(BF)
    linear = mm(normed_one, qkv_full) + bias_full.astype(F32)
    query = rotate(linear[:, :HD]).astype(BF)
    key = rotate(linear[:, HD : 2 * HD]).astype(BF)
    value = linear[:, 2 * HD :].astype(BF)
    scores = jnp.where(seen(), mm_nt(query, key) * score_scale, MASKED)
    exp_scores = jnp.exp(scores - jnp.max(scores, axis=1, keepdims=True))
    attn_probs = exp_scores / jnp.sum(exp_scores, axis=1, keepdims=True)
    probs_low = attn_probs.astype(BF)
    attn_head = mm(probs_low, value).astype(BF)

    by_head, ffn_blob = together(attn_head.reshape(seqs, rows, HD), ffn_blob)
    by_head = lax.all_to_all(by_head, SEQ, 0, 0, tiled=True)
    by_head, ffn_blob, dy_slots = together(by_head, ffn_blob, dy_slots)
    ffn_full = lax.all_gather(ffn_blob.reshape(seqs * depth, -1), "dp", axis=0, tiled=True)
    w_up = ffn_full[:, : 2 * units]
    w_down = ffn_full[:, 2 * units :]
    dy_slots = dy_slots.reshape(length, width + LANES)
    slots_all = dy_slots[:, width : width + experts].astype(jnp.int32)
    attn_flat = by_head.transpose(1, 0, 2).reshape(rows, heads * HD)
    attn_part = mm_nt(attn_flat, proj_rows)
    theirs = lax.dynamic_slice_in_dim(attn_part, (1 - me_tensor) * own, own, 0)
    attn_sum = mine(attn_part) + swap(theirs.astype(BF)).astype(F32)
    after_attn = x_own.astype(F32) + attn_sum
    scale_two = rms_scale(after_attn)
    norm_two = after_attn * scale_two
    normed_two = (norm_two * gain_ffn).astype(BF)
    h_all = plane_gather(normed_two)

    logits_all = mm(h_all, misc_full)
    router_probs = jax.nn.softmax(logits_all[:, 3 : 3 + experts], axis=-1)
    share_sig = jax.nn.sigmoid(logits_all[:, 2:3])
    mine_e = jnp.arange(experts, dtype=jnp.int32)[None, :] == me_seq
    slot_all = jnp.sum(jnp.where(mine_e, slots_all, 0), axis=1, keepdims=True)
    kept = slot_all < capacity
    gate_all = jnp.sum(jnp.where(mine_e, router_probs, 0.0), axis=1, keepdims=True)
    gate_all = jnp.where(kept, gate_all, 0.0)

    scales = jnp.pad(jnp.concatenate([gate_all, share_sig], 1), ((0, 0), (0, LANES - 2)))
    dgate_up, act_weighed, dots = feed_forward(h_all, dy_slots, ffn_full, scales)
    dots = jnp.concatenate([jnp.where(mine_e & kept, dots[:, 0:1], 0.0), dots[:, 1:2]], 1)
    dots = jnp.pad(dots, ((0, 0), (0, LANES - experts - 1)))
    back_parts = jnp.concatenate([mm_nt(dgate_up, w_up).astype(BF), dots.astype(BF)], 1)
    back_parts, act_weighed, dgate_up = together(back_parts, act_weighed, dgate_up)
    back = send_parts(back_parts)

    ffn_grad = ffn_grads(h_all, dy_slots, dgate_up, act_weighed)
    ffn_parts = mm_nt(act_weighed, w_down).astype(BF)
    back, ffn_parts, ffn_grad = together(back, ffn_parts, ffn_grad)
    back = sum_parts(back)
    ffn_grad = lax.psum_scatter(ffn_grad, "dp", scatter_dimension=0, tiled=True)

    probs_own = lax.dynamic_slice_in_dim(router_probs, me * own, own, 0)
    sig_own = lax.dynamic_slice_in_dim(share_sig, me * own, own, 0)
    dprobs = back[:, width : width + experts]
    dlogits = probs_own * (dprobs - jnp.sum(probs_own * dprobs, axis=1, keepdims=True))
    dshare = back[:, width + experts : width + experts + 1] * sig_own * (1.0 - sig_own)
    dmisc = jnp.concatenate([jnp.zeros((own, 2), F32), dshare, dlogits], 1)
    dmisc = jnp.pad(dmisc, ((0, 0), (0, LANES - n_misc))).astype(BF)
    dh_two = back[:, :width] + mm_nt(dmisc, misc_full)
    grad_misc = mm_tn(dmisc, normed_two)
    grad_gain_ffn = jnp.sum(dh_two * norm_two, axis=0)
    inner_two = dh_two * gain_ffn
    dx_one = dy_own.astype(F32) + scale_two * (
        inner_two - norm_two * jnp.mean(inner_two * norm_two, axis=-1, keepdims=True)
    )
    dx_low = dx_one.astype(BF)

    dx_pair = both_halves(dx_low)
    do_flat = mm(dx_pair, proj_rows).astype(BF)
    do_heads = do_flat.reshape(rows, heads, HD).transpose(1, 0, 2)
    do_head = lax.all_to_all(do_heads, SEQ, 0, 0, tiled=True).reshape(length, HD)
    dvalue = mm_tn(probs_low, do_head)
    dprob = mm_nt(do_head, value)
    row_delta = jnp.sum(attn_probs * dprob, axis=1, keepdims=True)
    dscore = (attn_probs * (dprob - row_delta)).astype(BF)
    dquery = mm(dscore, key) * score_scale
    dkey = mm_tn(dscore, query) * score_scale
    dlinear = jnp.concatenate([unrotate(dquery), unrotate(dkey), dvalue], 1).astype(BF)
    grad_bias = jnp.sum(dlinear.astype(F32), axis=0)
    dh_part = mm_nt(dlinear, qkv_full)
    grad_gain_attn = jnp.sum(dh_part * norm_one, axis=0)
    dh_sent = send_parts(dh_part)
    dh_sent, dlinear, ffn_parts, ffn_grad = together(dh_sent, dlinear, ffn_parts, ffn_grad)
    dh_one = sum_parts(dh_sent)

    bias_rows = grad_bias.reshape(3, dps * seqs, bias_part).transpose(1, 0, 2)
    bias_rows = bias_rows.reshape(dps * seqs, 3 * bias_part)
    bias_rows = jnp.pad(bias_rows, ((0, 0), (0, depth - 3 * bias_part))).reshape(1, width)
    small = jnp.concatenate(
        [grad_gain_attn[None], grad_gain_ffn[None], grad_misc[2:n_misc], bias_rows], 0
    )
    small = jnp.pad(small, ((0, LANES - n_misc - 1), (0, 0)))
    attn_grad = attn_grads(normed_one, dlinear, small, dx_pair, attn_flat)
    attn_grad = lax.psum_scatter(attn_grad, "dp", scatter_dimension=0, tiled=True)
    resid = x_own.astype(F32)
    scale_one = rms_scale(resid)
    norm_own = resid * scale_one
    inner_one = dh_one * gain_attn
    grad_in = dx_one + scale_one * (
        inner_one - norm_own * jnp.mean(inner_one * norm_own, axis=-1, keepdims=True)
    )
    grad_in = both_halves(grad_in)
    grad_in, ffn_grad = together(grad_in, ffn_grad)
    ffn_grad = lax.all_to_all(ffn_grad.reshape(seqs, depth, -1), SEQ, 0, 0, tiled=True)
    ffn_grad, ffn_parts = together(ffn_grad, ffn_parts)
    ffn_parts = send_parts(ffn_parts)
    ffn_parts, attn_grad = together(ffn_parts, attn_grad)
    hidden_out = both_halves((after_attn + sum_parts(ffn_parts)).astype(BF))
    attn_grad = attn_grad.reshape(seqs, depth, -1)
    attn_grad = lax.all_to_all(attn_grad, SEQ, 0, 0, tiled=True).astype(F32)

    def unit_columns(first, kind, size):
        at = [(2 * (first + i) + kind) * UNITS for i in range(up_to(size, UNITS) // UNITS)]
        picked = [
            ffn_grad[:, :, c : c + min(UNITS, size - i * UNITS)] for i, c in enumerate(at)
        ]
        return jnp.concatenate(picked, 2).astype(F32)

    shared_at = fe_pad // UNITS
    out_egu = jnp.stack([unit_columns(0, 0, fe), unit_columns(0, 1, fe)], 2).transpose(1, 0, 2, 3)
    out_sgu = [unit_columns(shared_at, kind, fs).transpose(1, 0, 2) for kind in (0, 1)]
    out_sgu = jnp.stack(out_sgu, 1).reshape(depth, 2, seqs * fs)
    down_at = 2 * units
    out_edn = ffn_grad[:, :, down_at : down_at + fe].transpose(0, 2, 1).astype(F32)
    out_sdn = ffn_grad[:, :, down_at + fe_pad : down_at + fe_pad + fs].transpose(0, 2, 1)
    out_sdn = out_sdn.reshape(seqs * fs, depth).astype(F32)
    out_qkv = attn_grad[:, :, : 3 * HD].reshape(heads, depth, 3, HD)
    out_qkv = out_qkv.transpose(1, 2, 0, 3).reshape(depth, 3, heads * HD)
    out_misc = jnp.sum(attn_grad[:, :, 3 * HD : 3 * HD + n_misc], axis=0)
    out_misc = out_misc + swap(out_misc)
    out_bias = attn_grad[:, : 3 * bias_part, 3 * HD + n_misc]
    out_bias = out_bias.reshape(heads, 3, bias_part).transpose(1, 0, 2)
    out_proj = jnp.sum(attn_grad[:, :, 3 * HD + LANES :], axis=0).T

    return (
        hidden_out[None],
        grad_in[None],
        out_misc[:, 0],
        out_qkv,
        out_bias,
        out_proj,
        out_misc[:, 1],
        out_misc[:, 3:n_misc],
        out_misc[:, 2],
        out_egu,
        out_edn,
        out_sgu,
        out_sdn,
    )


def solution(mesh):
    in_specs = (
        P("dp", SEQ, None),
        P("dp", SEQ, None),
        P("dp", SEQ, None),
        P("dp", SEQ, None),
        P("dp", None),
        P(("dp", *SEQ)),
        P(("dp", *SEQ), None, "tensor"),
        P(None, "tensor", ("dp", *SEQ)),
        P("tensor", ("dp", *SEQ)),
        P(("dp", *SEQ)),
        P(("dp", *SEQ), None),
        P(("dp", *SEQ)),
        P(("dp", *SEQ), None, None, "tensor"),
        P(None, "tensor", ("dp", *SEQ)),
        P(("dp", *SEQ), None, "tensor"),
        P("tensor", ("dp", *SEQ)),
    )
    out_specs = (
        P("dp", SEQ, None),
        P("dp", SEQ, None),
        P(("dp", *SEQ)),
        P(("dp", *SEQ), None, "tensor"),
        P(None, "tensor", ("dp", *SEQ)),
        P("tensor", ("dp", *SEQ)),
        P(("dp", *SEQ)),
        P(("dp", *SEQ), None),
        P(("dp", *SEQ)),
        P(("dp", *SEQ), None, None, "tensor"),
        P(None, "tensor", ("dp", *SEQ)),
        P(("dp", *SEQ), None, "tensor"),
        P("tensor", ("dp", *SEQ)),
    )
    fine = Mesh(mesh.devices.reshape(mesh.shape["dp"], 2, -1, 2), ("dp", *SEQ, "tensor"))
    return jax.shard_map(body, mesh=fine, in_specs=in_specs, out_specs=out_specs, check_vma=False)
```

profile of v0, /device:TPU:4, one launch (start us, length us, event | category | flops | bytes accessed | tf_op | source)
XLA Modules:
  0.0 646.4 jit_solution(6052922221656948183)
XLA Ops:
  11.6 8.2 %all-to-all-start = ((bf16[16,64,2048]{2,1,0:T(8,128)(2,1)}), bf16[16,64,2048]{2,1,0:T(8,128)(2,1)}, u32[]{:S(2)}, u32[]{:S(2)}) async-start(bf16[16,64,2048]{2,1,0:T(8,128)(2,1)} %broadcast_in_dim.152), calls=%async_computation | async-start | bytes 8388608 | tf_op jit(solution)/shard_map/all_to_all | solution.py:192
  28.5 49.9 %all-to-all-done = bf16[16,64,2048]{2,1,0:T(8,128)(2,1)} async-done(((bf16[16,64,2048]{2,1,0:T(8,128)(2,1)}), bf16[16,64,2048]{2,1,0:T(8,128)(2,1)}, u32[]{:S(2)}, u32[]{:S(2)}) %all-to-all-start) | async-done | bytes 4194336 | tf_op jit(solution)/shard_map/all_to_all | solution.py:192
  83.5 8.0 %all-to-all-done.1 = bf16[8,32,512]{2,1,0:T(8,128)(2,1)S(1)} async-done(((bf16[8,32,512]{2,1,0:T(8,128)(2,1)}), bf16[8,32,512]{2,1,0:T(8,128)(2,1)S(1)}, u32[]{:S(2)}, u32[]{:S(2)}) %all-to-all-start.1) | async-done | bytes 262176 | tf_op jit(solution)/shard_map/all_to_all | solution.py:311
  111.5 14.3 %all-to-all-done.2 = bf16[8,256,512]{1,2,0:T(8,128)(2,1)S(1)} async-done(((bf16[8,256,512]{1,2,0:T(8,128)(2,1)}), bf16[8,256,512]{1,2,0:T(8,128)(2,1)S(1)}, u32[]{:S(2)}, u32[]{:S(2)}) %all-to-all-start.2) | async-done | bytes 2097184 | tf_op jit(solution)/shard_map/all_to_all | solution.py:313
  146.6 12.6 %all-gather.8.cloned.1.call-start = ((), (), s32[]{:S(2)}) async-start(), calls=%async_computation.16 | async-start | bytes 15925248 | tf_op jit(solution)/shard_map/all_gather | solution.py:368
  168.8 16.8 %all-to-all-done.3 = bf16[8,32,3456]{2,1,0:T(8,128)(2,1)S(1)} async-done(((bf16[8,32,3456]{2,1,0:T(8,128)(2,1)}), bf16[8,32,3456]{2,1,0:T(8,128)(2,1)S(1)}, u32[]{:S(2)}, u32[]{:S(2)}) %all-to-all-start.3) | async-done | bytes 1769504 | tf_op jit(solution)/shard_map/all_to_all | solution.py:319
  185.6 17.2 %all_to_all.60 = bf16[8,128,128]{2,1,0:T(8,128)(2,1)S(1)} all-to-all(bf16[8,128,128]{2,1,0:T(8,128)(2,1)S(1)} %bitcast.175), channel_id=1, replica_groups=mesh['dp'=8,'z_hi'=2,'ring'=4,'tensor'=2] {'z_hi','ring'}, dimensions={0} | all-to-all | bytes 524288 | tf_op jit(solution)/shard_map/all_to_all | solution.py:366
  207.1 6.0 collective-permute-done.1
  221.8 52.8 %all-to-all-done.5 = bf16[16,64,2048]{2,1,0:T(8,128)(2,1)} async-done(((bf16[16,64,2048]{2,1,0:T(8,128)(2,1)}), bf16[16,64,2048]{2,1,0:T(8,128)(2,1)}, u32[]{:S(2)}, u32[]{:S(2)}) %all-to-all-start.5) | async-done | bytes 4194336 | tf_op jit(solution)/shard_map/all_to_all | solution.py:192
  281.8 24.6 %shard_map.255 = (bf16[1024,2304]{1,0:T(8,128)(2,1)}, bf16[1024,1152]{1,0:T(8,128)(2,1)}, f32[1024,128]{1,0:T(8,128)}) custom-call(bf16[1024,2048]{1,0:T(8,128)(2,1)} %bitcast.30.h_ref, bf16[1024,2176]{1,0:T(8,128)(2,1)} %bitcast.146, bf16[2048,3456]{1,0:T(8,128)(2,1)} %all-gather.8.cloned.1.call-done.up_ref.down_ref, ...), custom_call_target="tpu_custom_call" | custom-call | tf_op jit(solution)/shard_map/pallas_call | solution.py:110
  309.3 13.9 %fusion.13 = bf16[1024,2048]{1,0:T(8,128)(2,1)S(1)} fusion(bf16[1024,2304]{1,0:T(8,128)(2,1)} %get-tuple-element.57.middle_ref, bf16[2048,3456]{1,0:T(8,128)(2,1)} %all-gather.8.cloned.1.call-done.up_ref.down_ref), kind=kOutput, calls=%fused_computation.22 | convolution fusion | flops 9665773568 | bytes 18350080 | tf_op jit(solution)/shard_map/dot_general | solution.py:31
  325.7 4.9 all-to-all-start.6
  330.7 21.7 %shard_map.256 = bf16[2048,3456]{1,0:T(8,128)(2,1)} custom-call(bf16[1024,2048]{1,0:T(8,128)(2,1)} %bitcast.30.h_ref, bf16[1024,2176]{1,0:T(8,128)(2,1)} %bitcast.147, bf16[1024,2304]{1,0:T(8,128)(2,1)} %get-tuple-element.57.middle_ref, bf16[1024,1152]{1,0:T(8,128)(2,1)} %get-tuple-element.56.act_ref), custom_call_target="tpu_custom_call" | custom-call | tf_op jit(solution)/shard_map/pallas_call | solution.py:144
  352.4 9.6 %fusion.10 = bf16[1024,2048]{1,0:T(8,128)(2,1)} fusion(bf16[1024,1152]{1,0:T(8,128)(2,1)} %get-tuple-element.56.act_ref, bf16[2048,3456]{1,0:T(8,128)(2,1)} %all-gather.8.cloned.1.call-done.up_ref.down_ref), kind=kOutput, calls=%fused_computation.21 | convolution fusion | flops 4833935360 | bytes 11272192 | tf_op jit(solution)/shard_map/dot_general | solution.py:31
  361.9 28.0 %all-to-all-done.6 = bf16[16,64,2176]{2,1,0:T(8,128)(2,1)} async-done(((bf16[16,64,2176]{2,1,0:T(8,128)(2,1)}), bf16[16,64,2176]{2,1,0:T(8,128)(2,1)}, u32[]{:S(2)}, u32[]{:S(2)}) %all-to-all-start.6) | async-done | bytes 4456480 | tf_op jit(solution)/shard_map/all_to_all | solution.py:198
  397.3 7.0 %collective-permute-done.2 = bf16[64,2048]{1,0:T(8,128)(2,1)S(1)} collective-permute-done((bf16[64,2048]{1,0:T(8,128)(2,1)S(1)}, bf16[64,2048]{1,0:T(8,128)(2,1)S(1)}, u32[]{:S(2)}, u32[]{:S(2)}) %collective-permute-start.2) | collective-permute-done | bytes 262176 | tf_op jit(solution)/shard_map/ppermute | solution.py:64
  407.5 11.4 %all_to_all.61 = bf16[8,128,128]{2,1,0:T(8,128)(2,1)S(1)} all-to-all(bf16[8,128,128]{2,1,0:T(8,128)(2,1)S(1)} %bitcast.167), channel_id=1, replica_groups=mesh['dp'=8,'z_hi'=2,'ring'=4,'tensor'=2] {'z_hi','ring'}, dimensions={0} | all-to-all | bytes 524288 | tf_op jit(solution)/shard_map/all_to_all | solution.py:425
  430.4 6.4 fusion.5
  446.8 48.7 %all-to-all-done.8 = bf16[16,64,2048]{2,1,0:T(8,128)(2,1)} async-done(((bf16[16,64,2048]{2,1,0:T(8,128)(2,1)}), bf16[16,64,2048]{2,1,0:T(8,128)(2,1)}, u32[]{:S(2)}, u32[]{:S(2)}) %all-to-all-start.8) | async-done | bytes 4194336 | tf_op jit(solution)/shard_map/all_to_all | solution.py:198
  495.4 9.8 %shard_map.257 = bf16[2048,1536]{1,0:T(8,128)(2,1)} custom-call(bf16[1024,2048]{1,0:T(8,128)(2,1)} %copy-done, bf16[1024,384]{1,0:T(8,128)(2,1)} %copy-done.4, f32[128,2048]{1,0:T(8,128)} %select_maximum_fusion.small_ref, bf16[128,2048]{1,0:T(8,128)(2,1)} %pad_maximum_fusion.3.dx_ref, bf16[128,1024]{1,0:T(8,128)(2,1)} %copy_bitcast_fusion.2.heads_ref), custom_call_target="tpu_custom_call" | custom-call | tf_op jit(solution)/shard_map/pallas_call | solution.py:172
  509.5 11.6 %collective-permute-done.3 = f32[64,2048]{1,0:T(8,128)S(1)} collective-permute-done((f32[64,2048]{1,0:T(8,128)S(1)}, f32[64,2048]{1,0:T(8,128)S(1)}, u32[]{:S(2)}, u32[]{:S(2)}) %collective-permute-start.3) | collective-permute-done | bytes 524320 | tf_op jit(solution)/shard_map/ppermute | solution.py:64
  522.3 25.8 %all_to_all.62 = bf16[8,32,3456]{2,1,0:T(8,128)(2,1)S(1)} all-to-all(bf16[8,32,3456]{2,1,0:T(8,128)(2,1)S(1)} %bitcast.162), channel_id=1, replica_groups=mesh['dp'=8,'z_hi'=2,'ring'=4,'tensor'=2] {'z_hi','ring'}, dimensions={0} | all-to-all | bytes 3538944 | tf_op jit(solution)/shard_map/all_to_all | solution.py:458
  557.1 49.5 %all-to-all-done.10 = bf16[16,64,2048]{2,1,0:T(8,128)(2,1)} async-done(((bf16[16,64,2048]{2,1,0:T(8,128)(2,1)}), bf16[16,64,2048]{2,1,0:T(8,128)(2,1)}, u32[]{:S(2)}, u32[]{:S(2)}) %all-to-all-start.10) | async-done | bytes 4194336 | tf_op jit(solution)/shard_map/all_to_all | solution.py:198
  622.7 10.8 %all-to-all-done.11 = bf16[8,32,1536]{2,1,0:T(8,128)(2,1)S(1)} async-done(((bf16[8,32,1536]{2,1,0:T(8,128)(2,1)}), bf16[8,32,1536]{2,1,0:T(8,128)(2,1)S(1)}, u32[]{:S(2)}, u32[]{:S(2)}) %all-to-all-start.11) | async-done | bytes 786464 | tf_op jit(solution)/shard_map/all_to_all | solution.py:464
  (262 shorter events, 161.7 us)
Async XLA Ops:
  7.2 121.0 %all-gather.4.cloned.1.call-start = ((), (), s32[]{:S(2)}) async-start(), calls=%async_computation.14 | async-start | bytes 4259840 | tf_op jit(solution)/shard_map/all_gather | solution.py:308
  11.6 66.8 %all-to-all-start = ((bf16[16,64,2048]{2,1,0:T(8,128)(2,1)}), bf16[16,64,2048]{2,1,0:T(8,128)(2,1)}, u32[]{:S(2)}, u32[]{:S(2)}) async-start(bf16[16,64,2048]{2,1,0:T(8,128)(2,1)} %broadcast_in_dim.152), calls=%async_computation | async-start | bytes 8388608 | tf_op jit(solution)/shard_map/all_to_all | solution.py:192
  21.9 87.2 %collective-permute-start = (bf16[128,2176]{1,0:T(8,128)(2,1)}, bf16[128,2176]{1,0:T(8,128)(2,1)}, u32[]{:S(2)}, u32[]{:S(2)}) collective-permute-start(bf16[128,2176]{1,0:T(8,128)(2,1)} %fusion.43), channel_id=1, source_target_pairs={{0,9},{1,8},{2,11},{3,10},{4,13},{5,12},{6,15},{7,14},{8,1},{9,0},... | collective-permute-start | bytes 1671176 | tf_op jit(solution)/shard_map/ppermute | solution.py:60
  28.5 64.7 %copy-start.8 = (bf16[8,32,704]{2,1,0:T(8,128)(2,1)}, bf16[8,32,704]{2,1,0:T(8,128)(2,1)S(1)}, u32[]{:S(2)}) copy-start(bf16[8,32,704]{2,1,0:T(8,128)(2,1)S(1)} %get-tuple-element.234) | copy-start | bytes 1081348
  78.4 20.3 %copy-start.27 = (bf16[2816,32]{0,1:T(8,128)(2,1)S(1)}, bf16[2816,32]{0,1:T(8,128)(2,1)}, u32[]{:S(2)}) copy-start(bf16[2816,32]{0,1:T(8,128)(2,1)} %param.31) | copy-start | bytes 540676
  78.4 13.2 %all-to-all-start.1 = ((bf16[8,32,512]{2,1,0:T(8,128)(2,1)}), bf16[8,32,512]{2,1,0:T(8,128)(2,1)S(1)}, u32[]{:S(2)}, u32[]{:S(2)}) async-start(bf16[8,32,512]{2,1,0:T(8,128)(2,1)} %maximum_maximum_fusion), calls=%async_computation.1 | async-start | bytes 524288 | tf_op jit(solution)/shard_map/all_to_all | solution.py:311
  93.2 32.5 %all-to-all-start.2 = ((bf16[8,256,512]{1,2,0:T(8,128)(2,1)}), bf16[8,256,512]{1,2,0:T(8,128)(2,1)S(1)}, u32[]{:S(2)}, u32[]{:S(2)}) async-start(bf16[8,256,512]{1,2,0:T(8,128)(2,1)} %broadcast_in_dim.160), calls=%async_computation.2 | async-start | bytes 4194304 | tf_op jit(solution)/shard_map/all_to_all | solution.py:313
  98.0 104.8 %all-gather.6.cloned.1.call-start = ((), (), s32[]{:S(2)}) async-start(), calls=%async_computation.15 | async-start | bytes 5570560 | tf_op jit(solution)/shard_map/all_gather | solution.py:318
  110.3 17.9 %copy-start.32 = (s32[1,2]{1,0:T(1,128)S(1)}, s32[1,2]{1,0:T(1,128)}, u32[]{:S(2)}) copy-start(s32[1,2]{1,0:T(1,128)} %param.20) | copy-start | bytes 28
  142.1 43.5 %all-to-all-start.3 = ((bf16[8,32,3456]{2,1,0:T(8,128)(2,1)}), bf16[8,32,3456]{2,1,0:T(8,128)(2,1)S(1)}, u32[]{:S(2)}, u32[]{:S(2)}) async-start(bf16[8,32,3456]{2,1,0:T(8,128)(2,1)} %pad_dynamic-update-slice_fusion.1), calls=%async_computation.3 | async-start | bytes 3538944 | tf_op jit(solution)/shard_map/all_to_all | solution.py:319
  146.6 135.2 %all-gather.8.cloned.1.call-start = ((), (), s32[]{:S(2)}) async-start(), calls=%async_computation.16 | async-start | bytes 15925248 | tf_op jit(solution)/shard_map/all_gather | solution.py:368
  206.7 6.5 collective-permute-start.1
  216.0 58.6 %all-to-all-start.5 = ((bf16[16,64,2048]{2,1,0:T(8,128)(2,1)}), bf16[16,64,2048]{2,1,0:T(8,128)(2,1)}, u32[]{:S(2)}, u32[]{:S(2)}) async-start(bf16[16,64,2048]{2,1,0:T(8,128)(2,1)} %broadcast_in_dim.165), calls=%async_computation.5 | async-start | bytes 8388608 | tf_op jit(solution)/shard_map/all_to_all | solution.py:192
  325.7 64.2 %all-to-all-start.6 = ((bf16[16,64,2176]{2,1,0:T(8,128)(2,1)}), bf16[16,64,2176]{2,1,0:T(8,128)(2,1)}, u32[]{:S(2)}, u32[]{:S(2)}) async-start(bf16[16,64,2176]{2,1,0:T(8,128)(2,1)} %bitcast.148), calls=%async_computation.6 | async-start | bytes 8912896 | tf_op jit(solution)/shard_map/all_to_all | solution.py:198
  330.7 164.8 %reduce-scatter.3.cloned.1.call-start = ((), (), s32[]{:S(2)}) async-start(), calls=%async_computation.17 | async-start | bytes 15925248 | tf_op jit(solution)/shard_map/reduce_scatter | solution.py:404
  397.0 7.3 %collective-permute-start.2 = (bf16[64,2048]{1,0:T(8,128)(2,1)S(1)}, bf16[64,2048]{1,0:T(8,128)(2,1)S(1)}, u32[]{:S(2)}, u32[]{:S(2)}) collective-permute-start(bf16[64,2048]{1,0:T(8,128)(2,1)S(1)} %fusion.90), channel_id=1, source_target_pairs={{0,1},{1,0},{2,3},{3,2},{4,5},{5,4},{6,7},{7,6},{8,9},{9,8},{10,11... | collective-permute-start | bytes 786440 | tf_op jit(solution)/shard_map/ppermute | solution.py:64
  397.3 21.6 %copy-start.2 = (f32[1024,1024]{0,1:T(8,128)S(1)}, f32[1024,1024]{0,1:T(8,128)}, u32[]{:S(2)}) copy-start(f32[1024,1024]{0,1:T(8,128)} %copy-done.1) | copy-start | bytes 12582916
  436.8 58.6 %all-to-all-start.8 = ((bf16[16,64,2048]{2,1,0:T(8,128)(2,1)}), bf16[16,64,2048]{2,1,0:T(8,128)(2,1)}, u32[]{:S(2)}, u32[]{:S(2)}) async-start(bf16[16,64,2048]{2,1,0:T(8,128)(2,1)} %bitcast.159), calls=%async_computation.8 | async-start | bytes 8388608 | tf_op jit(solution)/shard_map/all_to_all | solution.py:198
  441.3 165.3 %reduce-scatter.5.cloned.1.call-start = ((), (), s32[]{:S(2)}) async-start(), calls=%async_computation.18 | async-start | bytes 7077888 | tf_op jit(solution)/shard_map/reduce_scatter | solution.py:448
  508.9 12.2 %collective-permute-start.3 = (f32[64,2048]{1,0:T(8,128)S(1)}, f32[64,2048]{1,0:T(8,128)S(1)}, u32[]{:S(2)}, u32[]{:S(2)}) collective-permute-start(f32[64,2048]{1,0:T(8,128)S(1)} %fusion.47), channel_id=1, source_target_pairs={{0,1},{1,0},{2,3},{3,2},{4,5},{5,4},{6,7},{7,6},{8,9},{9,8},{10,11... | collective-permute-start | bytes 1572872 | tf_op jit(solution)/shard_map/ppermute | solution.py:64
  548.0 58.6 %all-to-all-start.10 = ((bf16[16,64,2048]{2,1,0:T(8,128)(2,1)}), bf16[16,64,2048]{2,1,0:T(8,128)(2,1)}, u32[]{:S(2)}, u32[]{:S(2)}) async-start(bf16[16,64,2048]{2,1,0:T(8,128)(2,1)} %bitcast.158), calls=%async_computation.11 | async-start | bytes 8388608 | tf_op jit(solution)/shard_map/all_to_all | solution.py:198
  610.5 10.3 %collective-permute-start.4 = (bf16[64,2048]{1,0:T(8,128)(2,1)}, bf16[64,2048]{1,0:T(8,128)(2,1)}, u32[]{:S(2)}, u32[]{:S(2)}) collective-permute-start(bf16[64,2048]{1,0:T(8,128)(2,1)} %add_convert_fusion), channel_id=1, source_target_pairs={{0,1},{1,0},{2,3},{3,2},{4,5},{5,4},{6,7},{7,6},{8,9},{9,8},{10,11... | collective-permute-start | bytes 786440 | tf_op jit(solution)/shard_map/ppermute | solution.py:64
  617.3 16.3 %all-to-all-start.11 = ((bf16[8,32,1536]{2,1,0:T(8,128)(2,1)}), bf16[8,32,1536]{2,1,0:T(8,128)(2,1)S(1)}, u32[]{:S(2)}, u32[]{:S(2)}) async-start(bf16[8,32,1536]{2,1,0:T(8,128)(2,1)} %bitcast.169), calls=%async_computation.13 | async-start | bytes 1572864 | tf_op jit(solution)/shard_map/all_to_all | solution.py:464
  633.8 4.4 collective-permute-start.5
  (32 other events, 240.0 us)
Sparse Core Ops, SparseCore 0:
  11.3 104.7 all-gather.3
  128.3 69.0 all-gather.5
  202.9 70.8 all-gather.7
  390.1 74.5 reduce-scatter.2
  505.4 37.2 reduce-scatter.4
where the time goes:
time: 657 us; the launch traced here: 646 us
  waiting for transfers between devices  304 us (46%)
  starting transfers between devices  63.6 us (10%)
  Pallas kernels  56.1 us (9%)
  blocking collectives  54.4 us (8%)
  matrix products  54.3 us (8%)
  other arithmetic  50.9 us (8%)
  local copies, waits for them, and re-layouts  47.9 us (7%)
  between operations  15 us (2%)
    all_to_all x3, waiting for transfers between devices, send_parts(): return lax.all_to_all(parts, GRID, 0, 0, tiled=True)  126 us
    all_to_all x2, waiting for transfers between devices, plane_gather(): lax.all_to_all(copies, GRID, 0, 0, tiled=True).reshape(count * n, width)  103 us
    dot_general x15, matrix products, dot(): return lax.dot_general(a, b, (dims, ((), ())), preferred_element_type=F32)  54.3 us
    all_to_all x1, blocking collectives, body(): lax.all_to_all(ffn_grad.reshape(seqs, depth, -1), SEQ, 0, 0, tiled=True)  25.8 us
    ppermute x5, waiting for transfers between devices, swap(): return lax.ppermute(x, 'tensor', [(0, 1), (1, 0)])  24.6 us
    pallas_call x1, Pallas kernels, feed_forward(): pl.pallas_call(feed_forward_kernel, grid=(parts,), in_specs=[whole(width)...  24.6 us
    pallas_call x1, Pallas kernels, ffn_grads(): pl.pallas_call(ffn_grads_kernel, grid=(width // step,), in_specs=[pl.Bloc...  21.7 us
    unnamed x89, local copies, waits for them, and re-layouts  17.8 us
  transfers between devices with their start and end apart: 20, of which 12 were waited for; matrix products, arithmetic and copies ran while one was open for 19% of the time, Pallas kernels for 3%

commit v1 on v0

--- a/solution.py
+++ b/solution.py
@@ -1,3 +1,4 @@
+import functools
 import math
 
 import jax
@@ -69,91 +70,131 @@
 
 
 UNITS = 384
+EXPERTS = 8
+SHARE_AT = 2
+EXPERT_AT = 3
 VMEM = 56 * 1024 * 1024
 
 
-def feed_forward_kernel(h_ref, dy_ref, up_ref, down_ref, scale_ref, middle_ref, act_ref, dot_ref):
-    routed = pl.program_id(0) < pl.num_programs(0) - 1
-    tokens = h_ref.shape[0]
+def feed_forward_kernel(
+    capacity, expert_ref, h_ref, dy_ref, up_ref, down_ref, misc_ref,
+    middle_ref, act_ref, dot_ref, prob_ref, scale_ref,
+):
+    part = pl.program_id(0)
+    routed = part < pl.num_programs(0) - 1
+    tokens, width = h_ref.shape
+    expert = expert_ref[0]
     step = 256
-
-    @pl.when(pl.program_id(0) == 0)
+    lane = lax.broadcasted_iota(jnp.int32, (step, LANES), 1)
+
+    def column(x, at):
+        return jnp.sum(jnp.where(lane == at, x, 0.0), axis=1, keepdims=True)
+
+    @pl.when(part == 0)
     def _():
+        for at in range(0, tokens, step):
+            here = pl.ds(at, step)
+            logits = mm(h_ref[here, :], misc_ref[...])
+            among = (lane >= EXPERT_AT) & (lane < EXPERT_AT + EXPERTS)
+            top = jnp.max(jnp.where(among, logits, -jnp.inf), axis=1, keepdims=True)
+            raised = jnp.where(among, jnp.exp(jnp.where(among, logits - top, 0.0)), 0.0)
+            probs = raised / jnp.sum(raised, axis=1, keepdims=True)
+            share = jax.nn.sigmoid(column(logits, SHARE_AT))
+            slot = column(dy_ref[here, width:].astype(F32), expert)
+            gate = jnp.where(slot < capacity, column(probs, EXPERT_AT + expert), 0.0)
+            prob_ref[here, :] = jnp.where(lane == SHARE_AT, share, probs)
+            kept = jnp.where(slot < capacity, 1.0, 0.0)
+            scale_ref[here, :] = jnp.where(
+                lane == 0, gate, jnp.where(lane == 1, share, jnp.where(lane == 2, kept, 0.0))
+            )
         dot_ref[...] = jnp.zeros_like(dot_ref)
 
     for at in range(0, tokens, step):
         here = pl.ds(at, step)
         gate_up = mm(h_ref[here, :], up_ref[...])
-        back = mm(dy_ref[here, :], down_ref[...])
+        back = mm(dy_ref[here, :width], down_ref[...])
         gate, up = gate_up[:, :UNITS], gate_up[:, UNITS:]
         scale = jnp.where(routed, scale_ref[here, 0:1], scale_ref[here, 1:2])
+        counts = jnp.where(routed, scale_ref[here, 2:3], 1.0)
         sigma = jax.nn.sigmoid(gate)
         silu = gate * sigma
         act = (silu * up).astype(BF).astype(F32)
-        dots = jnp.sum(act * back, axis=1, keepdims=True)
-        place = lax.broadcasted_iota(jnp.int32, (step, LANES), 1)
-        place = place == jnp.where(routed, 0, 1)
-        dot_ref[here, :] += jnp.where(place, dots, 0.0)
+        dots = jnp.sum(act * back, axis=1, keepdims=True) * counts
+        dot_ref[here, :] += jnp.where(lane == jnp.where(routed, expert, EXPERTS), dots, 0.0)
         back = back * scale
         act_ref[here, :] = (act * scale).astype(BF)
         middle_ref[here, :UNITS] = (back * up * sigma * (1.0 + gate * (1.0 - sigma))).astype(BF)
         middle_ref[here, UNITS:] = (back * silu).astype(BF)
 
 
-def feed_forward(h, dy, weights, scales):
+def feed_forward(h, others, weights, misc, expert, capacity):
     tokens, width = h.shape
     parts = weights.shape[1] // (3 * UNITS)
 
-    def whole(columns):
-        return pl.BlockSpec((tokens, columns), lambda i: (0, 0), pipeline_mode=pl.Buffered(1))
+    def whole(shape):
+        return pl.BlockSpec(shape, lambda i, e: (0, 0), pipeline_mode=pl.Buffered(1))
 
     return pl.pallas_call(
-        feed_forward_kernel,
-        grid=(parts,),
-        in_specs=[
-            whole(width),
-            whole(width),
-            pl.BlockSpec((width, 2 * UNITS), lambda i: (0, i)),
-            pl.BlockSpec((width, UNITS), lambda i: (0, 2 * parts + i)),
-            whole(LANES),
-        ],
-        out_specs=[
-            pl.BlockSpec((tokens, 2 * UNITS), lambda i: (0, i)),
-            pl.BlockSpec((tokens, UNITS), lambda i: (0, i)),
-            pl.BlockSpec((tokens, LANES), lambda i: (0, 0)),
-        ],
+        functools.partial(feed_forward_kernel, capacity),
+        grid_spec=pltpu.PrefetchScalarGridSpec(
+            num_scalar_prefetch=1,
+            grid=(parts,),
+            in_specs=[
+                whole(h.shape),
+                whole((tokens, width + LANES)),
+                pl.BlockSpec((width, 2 * UNITS), lambda i, e: (0, i)),
+                pl.BlockSpec((width, UNITS), lambda i, e: (0, 2 * parts + i)),
+                whole(misc.shape),
+            ],
+            out_specs=[
+                pl.BlockSpec((tokens, 2 * UNITS), lambda i, e: (0, i)),
+                pl.BlockSpec((tokens, UNITS), lambda i, e: (0, i)),
+                pl.BlockSpec((tokens, LANES), lambda i, e: (0, 0)),
+                pl.BlockSpec((tokens, LANES), lambda i, e: (0, 0)),
+            ],
+            scratch_shapes=[pltpu.VMEM((tokens, LANES), F32)],
+        ),
         out_shape=[
             jax.ShapeDtypeStruct((tokens, 2 * UNITS * parts), BF),
             jax.ShapeDtypeStruct((tokens, UNITS * parts), BF),
             jax.ShapeDtypeStruct((tokens, LANES), F32),
+            jax.ShapeDtypeStruct((tokens, LANES), F32),
         ],
         compiler_params=pltpu.CompilerParams(vmem_limit_bytes=VMEM),
-    )(h, dy, weights, weights, scales)
-
-
-def ffn_grads_kernel(h_ref, dy_ref, middle_ref, act_ref, grad_ref):
+    )(expert, h, others, weights, weights, misc)
+
+
+def ffn_rest_kernel(h_ref, dy_ref, middle_ref, act_ref, down_ref, grad_ref, out_ref):
     ups = middle_ref.shape[1]
     grad_ref[:, :ups] = mm_tn(h_ref[...], middle_ref[...]).astype(BF)
     grad_ref[:, ups:] = mm_tn(dy_ref[...], act_ref[...]).astype(BF)
-
-
-def ffn_grads(h, dy, middle, act):
+    out_ref[...] = mm_nt(act_ref[...], down_ref[...]).astype(BF)
+
+
+def ffn_rest(h, dy, middle, act, weights):
     tokens, width = h.shape
     ups, downs = middle.shape[1], act.shape[1]
     step = 256
     return pl.pallas_call(
-        ffn_grads_kernel,
+        ffn_rest_kernel,
         grid=(width // step,),
         in_specs=[
             pl.BlockSpec((tokens, step), lambda i: (0, i)),
             pl.BlockSpec((tokens, step), lambda i: (0, i)),
             pl.BlockSpec((tokens, ups), lambda i: (0, 0)),
             pl.BlockSpec((tokens, downs), lambda i: (0, 0)),
+            pl.BlockSpec((step, downs), lambda i: (i, ups // downs)),
         ],
-        out_specs=pl.BlockSpec((step, ups + downs), lambda i: (i, 0)),
-        out_shape=jax.ShapeDtypeStruct((width, ups + downs), BF),
+        out_specs=[
+            pl.BlockSpec((step, ups + downs), lambda i: (i, 0)),
+            pl.BlockSpec((tokens, step), lambda i: (0, i)),
+        ],
+        out_shape=[
+            jax.ShapeDtypeStruct((width, ups + downs), BF),
+            jax.ShapeDtypeStruct((tokens, width), BF),
+        ],
         compiler_params=pltpu.CompilerParams(vmem_limit_bytes=VMEM),
-    )(h, dy, middle, act)
+    )(h, dy, middle, act, weights)
 
 
 def attn_grads_kernel(h_ref, linear_ref, small_ref, dx_ref, heads_ref, grad_ref):
@@ -262,9 +303,8 @@
     slot_of = jnp.sum(
         jnp.where(chosen, position.reshape(rows, TOPK)[:, :, None] - (LANES - 1), 0), axis=1
     ) + (LANES - 1)
-    slot_cols = jnp.pad(slot_of.astype(BF), ((0, 0), (0, LANES - experts)))
+    slot_cols = jnp.pad(mine(slot_of).astype(BF), ((0, 0), (0, LANES - experts)))
     dy_own = mine(grad_out[0])
-    dy_slots = jnp.concatenate([grad_out[0], slot_cols], 1)
     x_own = mine(hidden_in[0])
 
     misc = jnp.concatenate(
@@ -298,25 +338,27 @@
     columns += [padded(edn_blob, fe_pad), padded(sdn_blob, fs_pad)]
     ffn_blob = jnp.concatenate(columns, axis=2)
 
-    facing = from_facing(dy_slots)
     first_ring = lax.axis_index("z_hi") == 0
-    dy_slots = jnp.stack(
-        [jnp.where(first_ring, dy_slots, facing), jnp.where(first_ring, facing, dy_slots)]
-    )
-
-    x_all = plane_gather(x_own)
-    proj_rows = lax.all_gather(w_proj.T, ("dp", *SEQ), axis=0, tiled=True)
-
-    x_all, attn_blob = together(x_all, attn_blob)
+
+    def both_rings(block):
+        facing = from_facing(block)
+        return jnp.stack(
+            [jnp.where(first_ring, block, facing), jnp.where(first_ring, facing, block)]
+        )
+
+    x_all = lax.all_gather(both_rings(hidden_in[0]), "ring", axis=1, tiled=True)
+    x_all = x_all.reshape(length, width)
+
     attn_blob = lax.all_to_all(attn_blob, SEQ, 0, 0, tiled=True).reshape(1, seqs * depth, -1)
     attn_full = jnp.broadcast_to(attn_blob, (dps, *attn_blob.shape[1:]))
     attn_full = lax.all_to_all(attn_full, "dp", 0, 0, tiled=True).reshape(width, -1)
+    x_all, attn_full, proj_rows, dy_slots = together(
+        x_all, attn_full, w_proj.T, jnp.concatenate([dy_own, slot_cols], 1)
+    )
+    proj_rows = lax.all_gather(proj_rows, ("dp", *SEQ), axis=0, tiled=True)
     qkv_full = attn_full[:, : 3 * HD]
     misc_full = attn_full[:, 3 * HD :]
-
-    attn_full, ffn_blob, dy_slots, proj_rows = together(attn_full, ffn_blob, dy_slots, proj_rows)
-    dy_slots = lax.all_gather(dy_slots, "ring", axis=1, tiled=True)
-    ffn_blob = lax.all_to_all(ffn_blob, SEQ, 0, 0, tiled=True)
+    dy_slots = plane_gather(dy_slots)
 
     bias_full = misc_full[:, n_misc].reshape(dps * seqs, depth)[:, : 3 * bias_part]
     bias_full = bias_full.reshape(dps * seqs, 3, bias_part).transpose(1, 0, 2).reshape(1, 3 * HD)
@@ -362,14 +404,10 @@
     probs_low = attn_probs.astype(BF)
     attn_head = mm(probs_low, value).astype(BF)
 
-    by_head, ffn_blob = together(attn_head.reshape(seqs, rows, HD), ffn_blob)
+    by_head, dy_slots = together(attn_head.reshape(seqs, rows, HD), dy_slots)
     by_head = lax.all_to_all(by_head, SEQ, 0, 0, tiled=True)
-    by_head, ffn_blob, dy_slots = together(by_head, ffn_blob, dy_slots)
-    ffn_full = lax.all_gather(ffn_blob.reshape(seqs * depth, -1), "dp", axis=0, tiled=True)
-    w_up = ffn_full[:, : 2 * units]
-    w_down = ffn_full[:, 2 * units :]
-    dy_slots = dy_slots.reshape(length, width + LANES)
-    slots_all = dy_slots[:, width : width + experts].astype(jnp.int32)
+    by_head, ffn_blob = together(by_head, ffn_blob)
+    ffn_blob = lax.all_to_all(ffn_blob, SEQ, 0, 0, tiled=True)
     attn_flat = by_head.transpose(1, 0, 2).reshape(rows, heads * HD)
     attn_part = mm_nt(attn_flat, proj_rows)
     theirs = lax.dynamic_slice_in_dim(attn_part, (1 - me_tensor) * own, own, 0)
@@ -378,33 +416,29 @@
     scale_two = rms_scale(after_attn)
     norm_two = after_attn * scale_two
     normed_two = (norm_two * gain_ffn).astype(BF)
-    h_all = plane_gather(normed_two)
-
-    logits_all = mm(h_all, misc_full)
-    router_probs = jax.nn.softmax(logits_all[:, 3 : 3 + experts], axis=-1)
-    share_sig = jax.nn.sigmoid(logits_all[:, 2:3])
-    mine_e = jnp.arange(experts, dtype=jnp.int32)[None, :] == me_seq
-    slot_all = jnp.sum(jnp.where(mine_e, slots_all, 0), axis=1, keepdims=True)
-    kept = slot_all < capacity
-    gate_all = jnp.sum(jnp.where(mine_e, router_probs, 0.0), axis=1, keepdims=True)
-    gate_all = jnp.where(kept, gate_all, 0.0)
-
-    scales = jnp.pad(jnp.concatenate([gate_all, share_sig], 1), ((0, 0), (0, LANES - 2)))
-    dgate_up, act_weighed, dots = feed_forward(h_all, dy_slots, ffn_full, scales)
-    dots = jnp.concatenate([jnp.where(mine_e & kept, dots[:, 0:1], 0.0), dots[:, 1:2]], 1)
-    dots = jnp.pad(dots, ((0, 0), (0, LANES - experts - 1)))
+    normed_sent, ffn_blob = together(normed_two, ffn_blob)
+    ffn_full = lax.all_gather(ffn_blob.reshape(seqs * depth, -1), "dp", axis=0, tiled=True)
+    w_up = ffn_full[:, : 2 * units]
+    h_all = plane_gather(normed_sent)
+
+    expert = me_seq.astype(jnp.int32).reshape(1)
+    dgate_up, act_weighed, dots, router = feed_forward(
+        h_all, dy_slots, ffn_full, misc_full, expert, capacity
+    )
     back_parts = jnp.concatenate([mm_nt(dgate_up, w_up).astype(BF), dots.astype(BF)], 1)
     back_parts, act_weighed, dgate_up = together(back_parts, act_weighed, dgate_up)
     back = send_parts(back_parts)
 
-    ffn_grad = ffn_grads(h_all, dy_slots, dgate_up, act_weighed)
-    ffn_parts = mm_nt(act_weighed, w_down).astype(BF)
+    ffn_grad, ffn_parts = ffn_rest(h_all, dy_slots, dgate_up, act_weighed, ffn_full)
     back, ffn_parts, ffn_grad = together(back, ffn_parts, ffn_grad)
     back = sum_parts(back)
     ffn_grad = lax.psum_scatter(ffn_grad, "dp", scatter_dimension=0, tiled=True)
-
-    probs_own = lax.dynamic_slice_in_dim(router_probs, me * own, own, 0)
-    sig_own = lax.dynamic_slice_in_dim(share_sig, me * own, own, 0)
+    half = width // 2
+    ffn_left, ffn_right = ffn_parts[:, :half], ffn_parts[:, half:]
+
+    router_own = lax.dynamic_slice_in_dim(router, me * own, own, 0)
+    probs_own = router_own[:, EXPERT_AT : EXPERT_AT + experts]
+    sig_own = router_own[:, SHARE_AT : SHARE_AT + 1]
     dprobs = back[:, width : width + experts]
     dlogits = probs_own * (dprobs - jnp.sum(probs_own * dprobs, axis=1, keepdims=True))
     dshare = back[:, width + experts : width + experts + 1] * sig_own * (1.0 - sig_own)
@@ -423,6 +457,8 @@
     do_flat = mm(dx_pair, proj_rows).astype(BF)
     do_heads = do_flat.reshape(rows, heads, HD).transpose(1, 0, 2)
     do_head = lax.all_to_all(do_heads, SEQ, 0, 0, tiled=True).reshape(length, HD)
+    do_head, ffn_left = together(do_head, ffn_left)
+    ffn_left = send_parts(ffn_left)
     dvalue = mm_tn(probs_low, do_head)
     dprob = mm_nt(do_head, value)
     row_delta = jnp.sum(attn_probs * dprob, axis=1, keepdims=True)
@@ -433,9 +469,8 @@
     grad_bias = jnp.sum(dlinear.astype(F32), axis=0)
     dh_part = mm_nt(dlinear, qkv_full)
     grad_gain_attn = jnp.sum(dh_part * norm_one, axis=0)
-    dh_sent = send_parts(dh_part)
-    dh_sent, dlinear, ffn_parts, ffn_grad = together(dh_sent, dlinear, ffn_parts, ffn_grad)
-    dh_one = sum_parts(dh_sent)
+    dh_low, ffn_left = together(dh_part.astype(BF), ffn_left)
+    dh_sent = send_parts(dh_low)
 
     bias_rows = grad_bias.reshape(3, dps * seqs, bias_part).transpose(1, 0, 2)
     bias_rows = bias_rows.reshape(dps * seqs, 3 * bias_part)
@@ -445,7 +480,9 @@
     )
     small = jnp.pad(small, ((0, LANES - n_misc - 1), (0, 0)))
     attn_grad = attn_grads(normed_one, dlinear, small, dx_pair, attn_flat)
+    dh_sent, attn_grad, ffn_grad = together(dh_sent, attn_grad, ffn_grad)
     attn_grad = lax.psum_scatter(attn_grad, "dp", scatter_dimension=0, tiled=True)
+    dh_one = sum_parts(dh_sent)
     resid = x_own.astype(F32)
     scale_one = rms_scale(resid)
     norm_own = resid * scale_one
@@ -454,12 +491,12 @@
         inner_one - norm_own * jnp.mean(inner_one * norm_own, axis=-1, keepdims=True)
     )
     grad_in = both_halves(grad_in)
-    grad_in, ffn_grad = together(grad_in, ffn_grad)
     ffn_grad = lax.all_to_all(ffn_grad.reshape(seqs, depth, -1), SEQ, 0, 0, tiled=True)
-    ffn_grad, ffn_parts = together(ffn_grad, ffn_parts)
-    ffn_parts = send_parts(ffn_parts)
-    ffn_parts, attn_grad = together(ffn_parts, attn_grad)
-    hidden_out = both_halves((after_attn + sum_parts(ffn_parts)).astype(BF))
+    ffn_grad, ffn_right = together(ffn_grad, ffn_right)
+    ffn_right = send_parts(ffn_right)
+    ffn_right, attn_grad, grad_in = together(ffn_right, attn_grad, grad_in)
+    ffn_sum = jnp.concatenate([sum_parts(ffn_left), sum_parts(ffn_right)], 1)
+    hidden_out = both_halves((after_attn + ffn_sum).astype(BF))
     attn_grad = attn_grad.reshape(seqs, depth, -1)
     attn_grad = lax.all_to_all(attn_grad, SEQ, 0, 0, tiled=True).astype(F32)
 

time: 657 us -> 616 us (0.938)
  blocking collectives: 54.4 us -> 14.1 us
  matrix products: 54.3 us -> 39.4 us
  waiting for transfers between devices: 304 us -> 317 us
  Pallas kernels: 56.1 us -> 63.4 us
    all_to_all x3 -> x1, blocking collectives: 54.4 us -> 14.1 us  [body(): lax.all_to_all(attn_blob, SEQ, 0, 0, tiled=True)]
    all_to_all x3 -> x4, waiting for transfers between devices: 126 us -> 97.4 us  [send_parts(): return lax.all_to_all(parts, GRID, 0, 0, tiled=True)]
    all_to_all x1 -> x3, waiting for transfers between devices: 8.03 us -> 30.3 us  [the longest x1 17.9 us: body(): lax.all_to_all(ffn_grad.reshape(seqs, depth, -1), SEQ, 0, 0, tiled=True)]
    all_gather x2, waiting for transfers between devices: 0.01 us -> 21.6 us  [the longest x1 17.6 us: body(): proj_rows = lax.all_gather(proj_rows, ('dp', *SEQ), axis=0, tiled=True)]
    all_to_all x1, waiting for transfers between devices: 16.8 us -> 0.01 us  [body(): ffn_blob = lax.all_to_all(ffn_blob, SEQ, 0, 0, tiled=True)]
    dot_general x15 -> x13, matrix products: 54.3 us -> 39.4 us  [dot(): return lax.dot_general(a, b, (dims, ((), ())), preferred_element_type=F32)]
    all_gather x1, starting transfers between devices: 12.6 us -> 0.04 us  [body(): lax.all_gather(ffn_blob.reshape(seqs * depth, -1), 'dp', axis=0, tiled=True)]
    ppermute x1, waiting for transfers between devices: 0.01 us -> 12.1 us  [from_facing(): return lax.ppermute(x, GRID, [(i, i ^ flip) for i in range(count)])]
  transfers between devices with their start and end apart: 20 -> 23, of which waited for: 12 -> 17; matrix products, arithmetic and copies ran while one was open for 19% -> 17% of each run, Pallas kernels for 3% -> 6%
where the time goes in v1:
time: 616 us; the launch traced here: 609 us
  waiting for transfers between devices  317 us (51%)
  starting transfers between devices  66 us (11%)
  Pallas kernels  63.4 us (10%)
  other arithmetic  47.3 us (8%)
  local copies, waits for them, and re-layouts  46.9 us (8%)
  matrix products  39.4 us (6%)
  between operations  15 us (2%)
  blocking collectives  14.1 us (2%)
    all_to_all x2, waiting for transfers between devices, plane_gather(): lax.all_to_all(copies, GRID, 0, 0, tiled=True).reshape(count * n, width)  102 us
    all_to_all x4, waiting for transfers between devices, send_parts(): return lax.all_to_all(parts, GRID, 0, 0, tiled=True)  97.4 us
    dot_general x13, matrix products, dot(): return lax.dot_general(a, b, (dims, ((), ())), preferred_element_type=F32)  39.4 us
    pallas_call x1, Pallas kernels, ffn_rest(): pl.pallas_call(ffn_rest_kernel, grid=(width // step,), in_specs=[pl.Block...  26.9 us
    pallas_call x1, Pallas kernels, feed_forward(): pl.pallas_call(functools.partial(feed_forward_kernel, capacity), grid_spe...  26.6 us
    all_to_all x1, waiting for transfers between devices, body(): lax.all_to_all(attn_full, 'dp', 0, 0, tiled=True).reshape(width, -1)  22.1 us
    all_to_all x4, starting transfers between devices, send_parts(): return lax.all_to_all(parts, GRID, 0, 0, tiled=True)  20.1 us
    all_to_all x1, waiting for transfers between devices, body(): lax.all_to_all(ffn_grad.reshape(seqs, depth, -1), SEQ, 0, 0, tiled=True)  17.9 us
  transfers between devices with their start and end apart: 23, of which 17 were waited for; matrix products, arithmetic and copies ran while one was open for 17% of the time, Pallas kernels for 6%

profile of v1, /device:TPU:4, one launch (start us, length us, event | category | flops | bytes accessed | tf_op | source)
XLA Modules:
  0.0 609.1 jit_solution(8448735618412168273)
XLA Ops:
  11.4 12.1 %collective-permute-done = bf16[128,2048]{1,0:T(8,128)(2,1)S(1)} collective-permute-done((bf16[128,2048]{1,0:T(8,128)(2,1)}, bf16[128,2048]{1,0:T(8,128)(2,1)S(1)}, u32[]{:S(2)}, u32[]{:S(2)}) %collective-permute-start) | collective-permute-done | bytes 524320 | tf_op jit(solution)/shard_map/ppermute | solution.py:61
  26.9 14.1 %all_to_all.65 = bf16[8,32,512]{2,1,0:T(8,128)(2,1)S(1)} all-to-all(bf16[8,32,512]{2,1,0:T(8,128)(2,1)S(1)} %maximum_maximum_fusion), channel_id=1, replica_groups=mesh['dp'=8,'z_hi'=2,'ring'=4,'tensor'=2] {'z_hi','ring'}, dimensions={0} | all-to-all | bytes 524288 | tf_op jit(solution)/shard_map/all_to_all | solution.py:352
  42.5 4.9 all-to-all-start.1
  49.4 22.1 %all-to-all-done.1 = bf16[8,256,512]{2,1,0:T(8,128)(2,1)S(1)} async-done(((bf16[8,256,512]{2,1,0:T(8,128)(2,1)}), bf16[8,256,512]{2,1,0:T(8,128)(2,1)S(1)}, u32[]{:S(2)}, u32[]{:S(2)}) %all-to-all-start.1) | async-done | bytes 2097184 | tf_op jit(solution)/shard_map/all_to_all | solution.py:354
  85.7 6.4 %all-to-all-start.2 = ((bf16[16,64,2176]{2,1,0:T(8,128)(2,1)}), bf16[16,64,2176]{2,1,0:T(8,128)(2,1)}, u32[]{:S(2)}, u32[]{:S(2)}) async-start(bf16[16,64,2176]{2,1,0:T(8,128)(2,1)} %broadcast_in_dim.121), calls=%async_computation.2 | async-start | bytes 8912896 | tf_op jit(solution)/shard_map/all_to_all | solution.py:233
  108.8 45.5 %all-to-all-done.2 = bf16[16,64,2176]{2,1,0:T(8,128)(2,1)} async-done(((bf16[16,64,2176]{2,1,0:T(8,128)(2,1)}), bf16[16,64,2176]{2,1,0:T(8,128)(2,1)}, u32[]{:S(2)}, u32[]{:S(2)}) %all-to-all-start.2) | async-done | bytes 4456480 | tf_op jit(solution)/shard_map/all_to_all | solution.py:233
  160.1 8.4 %all-to-all-done.3 = bf16[8,128,128]{2,1,0:T(8,128)(2,1)S(1)} async-done(((bf16[8,128,128]{2,1,0:T(8,128)(2,1)}), bf16[8,128,128]{2,1,0:T(8,128)(2,1)S(1)}, u32[]{:S(2)}, u32[]{:S(2)}) %all-to-all-start.3) | async-done | bytes 262176 | tf_op jit(solution)/shard_map/all_to_all | solution.py:408
  172.8 17.6 %all-gather.6.cloned.1.call-done = bf16[2048,1024]{1,0:T(8,128)(2,1)} async-done(((bf16[32,1024]{1,0:T(8,128)(2,1)}), bf16[2048,1024]{1,0:T(8,128)(2,1)}) %all-gather.6.cloned.1.call-update) | async-done | bytes 4194320 | tf_op jit(solution)/shard_map/all_gather | solution.py:358
  195.4 7.8 %collective-permute-done.1 = bf16[64,2048]{1,0:T(8,128)(2,1)S(1)} collective-permute-done((bf16[64,2048]{1,0:T(8,128)(2,1)S(1)}, bf16[64,2048]{1,0:T(8,128)(2,1)S(1)}, u32[]{:S(2)}, u32[]{:S(2)}) %collective-permute-start.1) | collective-permute-done | bytes 262176 | tf_op jit(solution)/shard_map/ppermute | solution.py:65
  211.6 56.3 %all-to-all-done.5 = bf16[16,64,2048]{2,1,0:T(8,128)(2,1)} async-done(((bf16[16,64,2048]{2,1,0:T(8,128)(2,1)}), bf16[16,64,2048]{2,1,0:T(8,128)(2,1)}, u32[]{:S(2)}, u32[]{:S(2)}) %all-to-all-start.5) | async-done | bytes 4194336 | tf_op jit(solution)/shard_map/all_to_all | solution.py:233
  267.9 6.3 %all-gather.8.cloned.1.call-done.up_ref.down_ref = bf16[2048,3456]{1,0:T(8,128)(2,1)} async-done(((bf16[256,3456]{1,0:T(8,128)(2,1)}), bf16[2048,3456]{1,0:T(8,128)(2,1)}) %all-gather.8.cloned.1.call-update) | async-done | bytes 14155792 | tf_op jit(solution)/shard_map/all_gather | solution.py:420
  274.2 26.6 %shard_map.255 = (bf16[1024,2304]{1,0:T(8,128)(2,1)}, bf16[1024,1152]{1,0:T(8,128)(2,1)}, f32[1024,128]{1,0:T(8,128)}, f32[1024,128]{1,0:T(8,128)}) custom-call(s32[1]{0:T(128)} %bitcast.31.expert_ref, bf16[1024,2048]{1,0:T(8,128)(2,1)} %bitcast.32.h_ref, bf16[1024,2176]{1,0:T(8,128)(2,1)} %bitcast.21.dy_ref, ...), custom_call_target="tpu_custom_call" | custom-call | tf_op jit(solution)/shard_map/pallas_call | solution.py:137
  301.9 13.9 %fusion.8 = bf16[1024,2048]{1,0:T(8,128)(2,1)S(1)} fusion(bf16[1024,2304]{1,0:T(8,128)(2,1)} %get-tuple-element.61.middle_ref, bf16[2048,3456]{1,0:T(8,128)(2,1)} %all-gather.8.cloned.1.call-done.up_ref.down_ref), kind=kOutput, calls=%fused_computation.20 | convolution fusion | flops 9665773568 | bytes 18350080 | tf_op jit(solution)/shard_map/dot_general | solution.py:32
  318.3 7.0 %all-to-all-start.6 = ((bf16[16,64,2176]{2,1,0:T(8,128)(2,1)}), bf16[16,64,2176]{2,1,0:T(8,128)(2,1)}, u32[]{:S(2)}, u32[]{:S(2)}) async-start(bf16[16,64,2176]{2,1,0:T(8,128)(2,1)} %bitcast.149), calls=%async_computation.6 | async-start | bytes 8912896 | tf_op jit(solution)/shard_map/all_to_all | solution.py:239
  325.5 26.9 %shard_map.256 = (bf16[2048,3456]{1,0:T(8,128)(2,1)}, bf16[1024,2048]{1,0:T(8,128)(2,1)}) custom-call(bf16[1024,2048]{1,0:T(8,128)(2,1)} %bitcast.32.h_ref, bf16[1024,2176]{1,0:T(8,128)(2,1)} %bitcast.21.dy_ref, bf16[1024,2304]{1,0:T(8,128)(2,1)} %get-tuple-element.61.middle_ref, bf16[1024,1152]{1,0:T(8,128)(2,1)} %get-tuple-element.62.act_ref, ...), custom_call_target="tpu_custom_call" | custom-call | tf_op jit(solution)/shard_map/pallas_call | solution.py:178
  352.4 36.1 %all-to-all-done.6 = bf16[16,64,2176]{2,1,0:T(8,128)(2,1)} async-done(((bf16[16,64,2176]{2,1,0:T(8,128)(2,1)}), bf16[16,64,2176]{2,1,0:T(8,128)(2,1)}, u32[]{:S(2)}, u32[]{:S(2)}) %all-to-all-start.6) | async-done | bytes 4456480 | tf_op jit(solution)/shard_map/all_to_all | solution.py:239
  397.5 6.8 %collective-permute-done.2 = bf16[64,2048]{1,0:T(8,128)(2,1)S(1)} collective-permute-done((bf16[64,2048]{1,0:T(8,128)(2,1)S(1)}, bf16[64,2048]{1,0:T(8,128)(2,1)S(1)}, u32[]{:S(2)}, u32[]{:S(2)}) %collective-permute-start.2) | collective-permute-done | bytes 262176 | tf_op jit(solution)/shard_map/ppermute | solution.py:65
  439.3 5.8 fusion.5
  445.2 8.1 %all-to-all-done.8 = bf16[16,64,1024]{2,1,0:T(8,128)(2,1)} async-done(((bf16[16,64,1024]{2,1,0:T(8,128)(2,1)}), bf16[16,64,1024]{2,1,0:T(8,128)(2,1)}, u32[]{:S(2)}, u32[]{:S(2)}) %all-to-all-start.8) | async-done | bytes 2097184 | tf_op jit(solution)/shard_map/all_to_all | solution.py:239
  461.5 9.9 %shard_map.257 = bf16[2048,1536]{1,0:T(8,128)(2,1)} custom-call(bf16[1024,2048]{1,0:T(8,128)(2,1)} %copy-done, bf16[1024,384]{1,0:T(8,128)(2,1)} %copy-done.4, f32[128,2048]{1,0:T(8,128)} %select_maximum_fusion.small_ref, bf16[128,2048]{1,0:T(8,128)(2,1)} %pad_maximum_fusion.3.dx_ref, bf16[128,1024]{1,0:T(8,128)(2,1)} %copy_bitcast_fusion.2.heads_ref), custom_call_target="tpu_custom_call" | custom-call | tf_op jit(solution)/shard_map/pallas_call | solution.py:213
  471.4 36.5 %all-to-all-done.9 = bf16[16,64,2048]{2,1,0:T(8,128)(2,1)} async-done(((bf16[16,64,2048]{2,1,0:T(8,128)(2,1)}), bf16[16,64,2048]{2,1,0:T(8,128)(2,1)}, u32[]{:S(2)}, u32[]{:S(2)}) %all-to-all-start.9) | async-done | bytes 4194336 | tf_op jit(solution)/shard_map/all_to_all | solution.py:239
  518.0 17.9 %all-to-all-done.10 = bf16[8,32,3456]{2,1,0:T(8,128)(2,1)S(1)} async-done(((bf16[8,32,3456]{2,1,0:T(8,128)(2,1)}), bf16[8,32,3456]{2,1,0:T(8,128)(2,1)S(1)}, u32[]{:S(2)}, u32[]{:S(2)}) %all-to-all-start.10) | async-done | bytes 1769504 | tf_op jit(solution)/shard_map/all_to_all | solution.py:494
  554.5 16.6 %all-to-all-done.11 = bf16[16,64,1024]{2,1,0:T(8,128)(2,1)S(1)} async-done(((bf16[16,64,1024]{2,1,0:T(8,128)(2,1)}), bf16[16,64,1024]{2,1,0:T(8,128)(2,1)S(1)}, u32[]{:S(2)}, u32[]{:S(2)}) %all-to-all-start.11) | async-done | bytes 2097184 | tf_op jit(solution)/shard_map/all_to_all | solution.py:239
  585.8 10.8 %all-to-all-done.12 = bf16[8,32,1536]{2,1,0:T(8,128)(2,1)S(1)} async-done(((bf16[8,32,1536]{2,1,0:T(8,128)(2,1)}), bf16[8,32,1536]{2,1,0:T(8,128)(2,1)S(1)}, u32[]{:S(2)}, u32[]{:S(2)}) %all-to-all-start.12) | async-done | bytes 786464 | tf_op jit(solution)/shard_map/all_to_all | solution.py:501
  (267 shorter events, 169.6 us)
Async XLA Ops:
  7.2 68.2 %all-gather.4.cloned.1.call-start = ((), (), s32[]{:S(2)}) async-start(), calls=%async_computation.15 | async-start | bytes 5242880 | tf_op jit(solution)/shard_map/all_gather | solution.py:349
  7.3 16.3 %collective-permute-start = (bf16[128,2048]{1,0:T(8,128)(2,1)}, bf16[128,2048]{1,0:T(8,128)(2,1)S(1)}, u32[]{:S(2)}, u32[]{:S(2)}) collective-permute-start(bf16[128,2048]{1,0:T(8,128)(2,1)} %bitcast.162), channel_id=1, source_target_pairs={{0,9},{1,8},{2,11},{3,10},{4,13},{5,12},{6,15},{7,14},{8,1},{9,0},... | collective-permute-start | bytes 1572872 | tf_op jit(solution)/shard_map/ppermute | solution.py:61
  42.5 29.0 %all-to-all-start.1 = ((bf16[8,256,512]{2,1,0:T(8,128)(2,1)}), bf16[8,256,512]{2,1,0:T(8,128)(2,1)S(1)}, u32[]{:S(2)}, u32[]{:S(2)}) async-start(bf16[8,256,512]{2,1,0:T(8,128)(2,1)} %broadcast_in_dim.116), calls=%async_computation.1 | async-start | bytes 4194304 | tf_op jit(solution)/shard_map/all_to_all | solution.py:354
  47.4 143.1 %all-gather.6.cloned.1.call-start = ((), (), s32[]{:S(2)}) async-start(), calls=%async_computation.16 | async-start | bytes 4259840 | tf_op jit(solution)/shard_map/all_gather | solution.py:358
  85.7 68.6 %all-to-all-start.2 = ((bf16[16,64,2176]{2,1,0:T(8,128)(2,1)}), bf16[16,64,2176]{2,1,0:T(8,128)(2,1)}, u32[]{:S(2)}, u32[]{:S(2)}) async-start(bf16[16,64,2176]{2,1,0:T(8,128)(2,1)} %broadcast_in_dim.121), calls=%async_computation.2 | async-start | bytes 8912896 | tf_op jit(solution)/shard_map/all_to_all | solution.py:233
  107.2 51.3 %copy-start.29 = (bf16[8,704,32]{1,2,0:T(8,128)(2,1)S(1)}, bf16[8,704,32]{1,2,0:T(8,128)(2,1)}, u32[]{:S(2)}) copy-start(bf16[8,704,32]{1,2,0:T(8,128)(2,1)} %param.29) | copy-start | bytes 1081348
  154.2 14.2 %all-to-all-start.3 = ((bf16[8,128,128]{2,1,0:T(8,128)(2,1)}), bf16[8,128,128]{2,1,0:T(8,128)(2,1)S(1)}, u32[]{:S(2)}, u32[]{:S(2)}) async-start(bf16[8,128,128]{2,1,0:T(8,128)(2,1)} %bitcast.176), calls=%async_computation.3 | async-start | bytes 524288 | tf_op jit(solution)/shard_map/all_to_all | solution.py:408
  168.5 35.1 %all-to-all-start.4 = ((bf16[8,32,3456]{2,1,0:T(8,128)(2,1)}), bf16[8,32,3456]{2,1,0:T(8,128)(2,1)}, u32[]{:S(2)}, u32[]{:S(2)}) async-start(bf16[8,32,3456]{2,1,0:T(8,128)(2,1)} %pad_dynamic-update-slice_fusion.1), calls=%async_computation.4 | async-start | bytes 3538944 | tf_op jit(solution)/shard_map/all_to_all | solution.py:410
  172.8 101.4 %all-gather.8.cloned.1.call-start = ((), (), s32[]{:S(2)}) async-start(), calls=%async_computation.17 | async-start | bytes 15925248 | tf_op jit(solution)/shard_map/all_gather | solution.py:420
  194.2 9.0 %collective-permute-start.1 = (bf16[64,2048]{1,0:T(8,128)(2,1)S(1)}, bf16[64,2048]{1,0:T(8,128)(2,1)S(1)}, u32[]{:S(2)}, u32[]{:S(2)}) collective-permute-start(bf16[64,2048]{1,0:T(8,128)(2,1)S(1)} %dynamic-slice_convert_fusion), channel_id=1, source_target_pairs={{0,1},{1,0},{2,3},{3,2},{4,5},{5,4},{6,7},{7,6},{8,9},{9,8},{10,11... | collective-permute-start | bytes 786440 | tf_op jit(solution)/shard_map/ppermute | solution.py:65
  206.1 61.8 %all-to-all-start.5 = ((bf16[16,64,2048]{2,1,0:T(8,128)(2,1)}), bf16[16,64,2048]{2,1,0:T(8,128)(2,1)}, u32[]{:S(2)}, u32[]{:S(2)}) async-start(bf16[16,64,2048]{2,1,0:T(8,128)(2,1)} %broadcast_in_dim.122), calls=%async_computation.5 | async-start | bytes 8388608 | tf_op jit(solution)/shard_map/all_to_all | solution.py:233
  318.3 70.3 %all-to-all-start.6 = ((bf16[16,64,2176]{2,1,0:T(8,128)(2,1)}), bf16[16,64,2176]{2,1,0:T(8,128)(2,1)}, u32[]{:S(2)}, u32[]{:S(2)}) async-start(bf16[16,64,2176]{2,1,0:T(8,128)(2,1)} %bitcast.149), calls=%async_computation.6 | async-start | bytes 8912896 | tf_op jit(solution)/shard_map/all_to_all | solution.py:239
  325.3 182.6 %reduce-scatter.3.cloned.1.call-start = ((), (), s32[]{:S(2)}) async-start(), calls=%async_computation.18 | async-start | bytes 15925248 | tf_op jit(solution)/shard_map/reduce_scatter | solution.py:435
  396.9 7.4 %collective-permute-start.2 = (bf16[64,2048]{1,0:T(8,128)(2,1)S(1)}, bf16[64,2048]{1,0:T(8,128)(2,1)S(1)}, u32[]{:S(2)}, u32[]{:S(2)}) collective-permute-start(bf16[64,2048]{1,0:T(8,128)(2,1)S(1)} %fusion.76), channel_id=1, source_target_pairs={{0,1},{1,0},{2,3},{3,2},{4,5},{5,4},{6,7},{7,6},{8,9},{9,8},{10,11... | collective-permute-start | bytes 786440 | tf_op jit(solution)/shard_map/ppermute | solution.py:65
  408.8 12.9 %all-to-all-start.7 = ((bf16[8,128,128]{2,1,0:T(8,128)(2,1)}), bf16[8,128,128]{2,1,0:T(8,128)(2,1)S(1)}, u32[]{:S(2)}, u32[]{:S(2)}) async-start(bf16[8,128,128]{2,1,0:T(8,128)(2,1)} %bitcast.145), calls=%async_computation.7 | async-start | bytes 524288 | tf_op jit(solution)/shard_map/all_to_all | solution.py:459
  421.7 31.6 %all-to-all-start.8 = ((bf16[16,64,1024]{2,1,0:T(8,128)(2,1)}), bf16[16,64,1024]{2,1,0:T(8,128)(2,1)}, u32[]{:S(2)}, u32[]{:S(2)}) async-start(bf16[16,64,1024]{2,1,0:T(8,128)(2,1)} %bitcast.160), calls=%async_computation.8 | async-start | bytes 4194304 | tf_op jit(solution)/shard_map/all_to_all | solution.py:239
  453.3 54.6 %all-to-all-start.9 = ((bf16[16,64,2048]{2,1,0:T(8,128)(2,1)}), bf16[16,64,2048]{2,1,0:T(8,128)(2,1)}, u32[]{:S(2)}, u32[]{:S(2)}) async-start(bf16[16,64,2048]{2,1,0:T(8,128)(2,1)} %bitcast.161), calls=%async_computation.9 | async-start | bytes 8388608 | tf_op jit(solution)/shard_map/all_to_all | solution.py:239
  458.0 113.1 %reduce-scatter.5.cloned.1.call-start = ((), (), s32[]{:S(2)}) async-start(), calls=%async_computation.19 | async-start | bytes 7077888 | tf_op jit(solution)/shard_map/reduce_scatter | solution.py:484
  508.0 27.9 %all-to-all-start.10 = ((bf16[8,32,3456]{2,1,0:T(8,128)(2,1)}), bf16[8,32,3456]{2,1,0:T(8,128)(2,1)S(1)}, u32[]{:S(2)}, u32[]{:S(2)}) async-start(bf16[8,32,3456]{2,1,0:T(8,128)(2,1)} %bitcast.165), calls=%async_computation.11 | async-start | bytes 3538944 | tf_op jit(solution)/shard_map/all_to_all | solution.py:494
  517.2 26.6 %collective-permute-start.3 = (f32[64,2048]{1,0:T(8,128)}, f32[64,2048]{1,0:T(8,128)S(1)}, u32[]{:S(2)}, u32[]{:S(2)}) collective-permute-start(f32[64,2048]{1,0:T(8,128)} %fusion.41), channel_id=1, source_target_pairs={{0,1},{1,0},{2,3},{3,2},{4,5},{5,4},{6,7},{7,6},{8,9},{9,8},{10,11... | collective-permute-start | bytes 1572872 | tf_op jit(solution)/shard_map/ppermute | solution.py:65
  537.2 33.9 %all-to-all-start.11 = ((bf16[16,64,1024]{2,1,0:T(8,128)(2,1)}), bf16[16,64,1024]{2,1,0:T(8,128)(2,1)S(1)}, u32[]{:S(2)}, u32[]{:S(2)}) async-start(bf16[16,64,1024]{2,1,0:T(8,128)(2,1)} %bitcast.159), calls=%async_computation.12 | async-start | bytes 4194304 | tf_op jit(solution)/shard_map/all_to_all | solution.py:239
  572.5 12.3 %collective-permute-start.4 = (bf16[64,2048]{1,0:T(8,128)(2,1)S(1)}, bf16[64,2048]{1,0:T(8,128)(2,1)S(1)}, u32[]{:S(2)}, u32[]{:S(2)}) collective-permute-start(bf16[64,2048]{1,0:T(8,128)(2,1)S(1)} %fusion.59), channel_id=1, source_target_pairs={{0,1},{1,0},{2,3},{3,2},{4,5},{5,4},{6,7},{7,6},{8,9},{9,8},{10,11... | collective-permute-start | bytes 786440 | tf_op jit(solution)/shard_map/ppermute | solution.py:65
  581.3 15.2 %all-to-all-start.12 = ((bf16[8,32,1536]{2,1,0:T(8,128)(2,1)}), bf16[8,32,1536]{2,1,0:T(8,128)(2,1)S(1)}, u32[]{:S(2)}, u32[]{:S(2)}) async-start(bf16[8,32,1536]{2,1,0:T(8,128)(2,1)} %bitcast.47), calls=%async_computation.14 | async-start | bytes 1572864 | tf_op jit(solution)/shard_map/all_to_all | solution.py:501
  596.7 4.2 collective-permute-start.5
  (41 other events, 408.5 us)
Sparse Core Ops, SparseCore 0:
  25.9 49.5 all-gather.3
  78.7 111.7 all-gather.5
  203.7 70.4 all-gather.7
  388.7 76.1 reduce-scatter.2
  508.1 39.4 reduce-scatter.4

commit v2 on v1

--- a/solution.py
+++ b/solution.py
@@ -352,12 +352,12 @@
     attn_blob = lax.all_to_all(attn_blob, SEQ, 0, 0, tiled=True).reshape(1, seqs * depth, -1)
     attn_full = jnp.broadcast_to(attn_blob, (dps, *attn_blob.shape[1:]))
     attn_full = lax.all_to_all(attn_full, "dp", 0, 0, tiled=True).reshape(width, -1)
-    x_all, attn_full, proj_rows, dy_slots = together(
-        x_all, attn_full, w_proj.T, jnp.concatenate([dy_own, slot_cols], 1)
-    )
+    x_all, attn_full, proj_rows, ffn_blob = together(x_all, attn_full, w_proj.T, ffn_blob)
     proj_rows = lax.all_gather(proj_rows, ("dp", *SEQ), axis=0, tiled=True)
     qkv_full = attn_full[:, : 3 * HD]
     misc_full = attn_full[:, 3 * HD :]
+    ffn_blob = lax.all_to_all(ffn_blob, SEQ, 0, 0, tiled=True)
+    ffn_blob, dy_slots = together(ffn_blob, jnp.concatenate([dy_own, slot_cols], 1))
     dy_slots = plane_gather(dy_slots)
 
     bias_full = misc_full[:, n_misc].reshape(dps * seqs, depth)[:, : 3 * bias_part]
@@ -407,7 +407,8 @@
     by_head, dy_slots = together(attn_head.reshape(seqs, rows, HD), dy_slots)
     by_head = lax.all_to_all(by_head, SEQ, 0, 0, tiled=True)
     by_head, ffn_blob = together(by_head, ffn_blob)
-    ffn_blob = lax.all_to_all(ffn_blob, SEQ, 0, 0, tiled=True)
+    ffn_full = lax.all_gather(ffn_blob.reshape(seqs * depth, -1), "dp", axis=0, tiled=True)
+    w_up = ffn_full[:, : 2 * units]
     attn_flat = by_head.transpose(1, 0, 2).reshape(rows, heads * HD)
     attn_part = mm_nt(attn_flat, proj_rows)
     theirs = lax.dynamic_slice_in_dim(attn_part, (1 - me_tensor) * own, own, 0)
@@ -416,25 +417,24 @@
     scale_two = rms_scale(after_attn)
     norm_two = after_attn * scale_two
     normed_two = (norm_two * gain_ffn).astype(BF)
-    normed_sent, ffn_blob = together(normed_two, ffn_blob)
-    ffn_full = lax.all_gather(ffn_blob.reshape(seqs * depth, -1), "dp", axis=0, tiled=True)
-    w_up = ffn_full[:, : 2 * units]
-    h_all = plane_gather(normed_sent)
+    h_all = plane_gather(normed_two)
 
     expert = me_seq.astype(jnp.int32).reshape(1)
     dgate_up, act_weighed, dots, router = feed_forward(
         h_all, dy_slots, ffn_full, misc_full, expert, capacity
     )
     back_parts = jnp.concatenate([mm_nt(dgate_up, w_up).astype(BF), dots.astype(BF)], 1)
-    back_parts, act_weighed, dgate_up = together(back_parts, act_weighed, dgate_up)
+    half = width // 2
+    ffn_left = send_parts(mm_nt(act_weighed, ffn_full[:half, 2 * units :]))
+    back_parts, act_weighed, dgate_up, ffn_left = together(
+        back_parts, act_weighed, dgate_up, ffn_left
+    )
     back = send_parts(back_parts)
 
     ffn_grad, ffn_parts = ffn_rest(h_all, dy_slots, dgate_up, act_weighed, ffn_full)
     back, ffn_parts, ffn_grad = together(back, ffn_parts, ffn_grad)
     back = sum_parts(back)
     ffn_grad = lax.psum_scatter(ffn_grad, "dp", scatter_dimension=0, tiled=True)
-    half = width // 2
-    ffn_left, ffn_right = ffn_parts[:, :half], ffn_parts[:, half:]
 
     router_own = lax.dynamic_slice_in_dim(router, me * own, own, 0)
     probs_own = router_own[:, EXPERT_AT : EXPERT_AT + experts]
@@ -457,8 +457,8 @@
     do_flat = mm(dx_pair, proj_rows).astype(BF)
     do_heads = do_flat.reshape(rows, heads, HD).transpose(1, 0, 2)
     do_head = lax.all_to_all(do_heads, SEQ, 0, 0, tiled=True).reshape(length, HD)
-    do_head, ffn_left = together(do_head, ffn_left)
-    ffn_left = send_parts(ffn_left)
+    do_head, ffn_right = together(do_head, ffn_parts[:, half:])
+    ffn_right = send_parts(ffn_right)
     dvalue = mm_tn(probs_low, do_head)
     dprob = mm_nt(do_head, value)
     row_delta = jnp.sum(attn_probs * dprob, axis=1, keepdims=True)
@@ -469,8 +469,10 @@
     grad_bias = jnp.sum(dlinear.astype(F32), axis=0)
     dh_part = mm_nt(dlinear, qkv_full)
     grad_gain_attn = jnp.sum(dh_part * norm_one, axis=0)
-    dh_low, ffn_left = together(dh_part.astype(BF), ffn_left)
+    dh_low, ffn_right = together(dh_part.astype(BF), ffn_right)
     dh_sent = send_parts(dh_low)
+    ffn_sum = jnp.concatenate([sum_parts(ffn_left), sum_parts(ffn_right)], 1)
+    hidden_out = both_halves((after_attn + ffn_sum).astype(BF))
 
     bias_rows = grad_bias.reshape(3, dps * seqs, bias_part).transpose(1, 0, 2)
     bias_rows = bias_rows.reshape(dps * seqs, 3 * bias_part)
@@ -480,7 +482,9 @@
     )
     small = jnp.pad(small, ((0, LANES - n_misc - 1), (0, 0)))
     attn_grad = attn_grads(normed_one, dlinear, small, dx_pair, attn_flat)
-    dh_sent, attn_grad, ffn_grad = together(dh_sent, attn_grad, ffn_grad)
+    dh_sent, attn_grad, ffn_grad, hidden_out = together(
+        dh_sent, attn_grad, ffn_grad, hidden_out
+    )
     attn_grad = lax.psum_scatter(attn_grad, "dp", scatter_dimension=0, tiled=True)
     dh_one = sum_parts(dh_sent)
     resid = x_own.astype(F32)
@@ -492,11 +496,7 @@
     )
     grad_in = both_halves(grad_in)
     ffn_grad = lax.all_to_all(ffn_grad.reshape(seqs, depth, -1), SEQ, 0, 0, tiled=True)
-    ffn_grad, ffn_right = together(ffn_grad, ffn_right)
-    ffn_right = send_parts(ffn_right)
-    ffn_right, attn_grad, grad_in = together(ffn_right, attn_grad, grad_in)
-    ffn_sum = jnp.concatenate([sum_parts(ffn_left), sum_parts(ffn_right)], 1)
-    hidden_out = both_halves((after_attn + ffn_sum).astype(BF))
+    ffn_grad, attn_grad, grad_in = together(ffn_grad, attn_grad, grad_in)
     attn_grad = attn_grad.reshape(seqs, depth, -1)
     attn_grad = lax.all_to_all(attn_grad, SEQ, 0, 0, tiled=True).astype(F32)
 

time: 616 us -> 604 us (0.981)
  waiting for transfers between devices: 317 us -> 299 us
  blocking collectives: 14.1 us -> 27.4 us
  other arithmetic: 47.3 us -> 39.5 us
    ppermute x5, waiting for transfers between devices: 14.6 us -> 56 us  [swap(): return lax.ppermute(x, 'tensor', [(0, 1), (1, 0)])]
    all_to_all x4, waiting for transfers between devices: 97.4 us -> 65.2 us  [send_parts(): return lax.all_to_all(parts, GRID, 0, 0, tiled=True)]
    all_to_all x1, waiting for transfers between devices: 0.01 us -> 25.2 us  [body(): ffn_blob = lax.all_to_all(ffn_blob, SEQ, 0, 0, tiled=True)]
    all_to_all x1, waiting for transfers between devices: 17.9 us -> 0.01 us  [body(): lax.all_to_all(ffn_grad.reshape(seqs, depth, -1), SEQ, 0, 0, tiled=True)]
    all_gather x1, waiting for transfers between devices: 17.6 us -> 1.77 us  [body(): proj_rows = lax.all_gather(proj_rows, ('dp', *SEQ), axis=0, tiled=True)]
    all_to_all x0 -> x1, blocking collectives: none -> 13.3 us  [body(): by_head = lax.all_to_all(by_head, SEQ, 0, 0, tiled=True)]
    all_to_all x1, waiting for transfers between devices: 22.1 us -> 11.2 us  [body(): lax.all_to_all(attn_full, 'dp', 0, 0, tiled=True).reshape(width, -1)]
    all_to_all x1 -> x0, waiting for transfers between devices: 8.39 us -> none  [body(): by_head = lax.all_to_all(by_head, SEQ, 0, 0, tiled=True)]
  transfers between devices with their start and end apart: 23 -> 22, of which waited for: 17 -> 19; matrix products, arithmetic and copies ran while one was open for 17% -> 19% of each run, Pallas kernels for 6% -> 6%
where the time goes in v2:
time: 604 us; the launch traced here: 599 us
  waiting for transfers between devices  299 us (50%)
  starting transfers between devices  64.5 us (11%)
  Pallas kernels  63.3 us (10%)
  matrix products  45.3 us (8%)
  local copies, waits for them, and re-layouts  44.2 us (7%)
  other arithmetic  39.5 us (7%)
  blocking collectives  27.4 us (5%)
  between operations  15.3 us (3%)
    all_to_all x2, waiting for transfers between devices, plane_gather(): lax.all_to_all(copies, GRID, 0, 0, tiled=True).reshape(count * n, width)  106 us
    all_to_all x4, waiting for transfers between devices, send_parts(): return lax.all_to_all(parts, GRID, 0, 0, tiled=True)  65.2 us
    ppermute x5, waiting for transfers between devices, swap(): return lax.ppermute(x, 'tensor', [(0, 1), (1, 0)])  56 us
    dot_general x14, matrix products, dot(): return lax.dot_general(a, b, (dims, ((), ())), preferred_element_type=F32)  45.3 us
    pallas_call x1, Pallas kernels, ffn_rest(): pl.pallas_call(ffn_rest_kernel, grid=(width // step,), in_specs=[pl.Block...  26.9 us
    pallas_call x1, Pallas kernels, feed_forward(): pl.pallas_call(functools.partial(feed_forward_kernel, capacity), grid_spe...  26.6 us
    all_to_all x1, waiting for transfers between devices, body(): ffn_blob = lax.all_to_all(ffn_blob, SEQ, 0, 0, tiled=True)  25.2 us
    all_to_all x4, starting transfers between devices, send_parts(): return lax.all_to_all(parts, GRID, 0, 0, tiled=True)  18.7 us
  transfers between devices with their start and end apart: 22, of which 19 were waited for; matrix products, arithmetic and copies ran while one was open for 19% of the time, Pallas kernels for 6%

profile of v2, /device:TPU:4, one launch (start us, length us, event | category | flops | bytes accessed | tf_op | source)
XLA Modules:
  0.0 598.6 jit_solution(12645462969132872046)
XLA Ops:
  11.4 12.1 %collective-permute-done = bf16[128,2048]{1,0:T(8,128)(2,1)S(1)} collective-permute-done((bf16[128,2048]{1,0:T(8,128)(2,1)}, bf16[128,2048]{1,0:T(8,128)(2,1)S(1)}, u32[]{:S(2)}, u32[]{:S(2)}) %collective-permute-start) | collective-permute-done | bytes 524320 | tf_op jit(solution)/shard_map/ppermute | solution.py:61
  26.8 14.1 %all_to_all.65 = bf16[8,32,512]{2,1,0:T(8,128)(2,1)S(1)} all-to-all(bf16[8,32,512]{2,1,0:T(8,128)(2,1)S(1)} %maximum_maximum_fusion), channel_id=1, replica_groups=mesh['dp'=8,'z_hi'=2,'ring'=4,'tensor'=2] {'z_hi','ring'}, dimensions={0} | all-to-all | bytes 524288 | tf_op jit(solution)/shard_map/all_to_all | solution.py:352
  60.0 11.2 %all-to-all-done.1 = bf16[8,256,512]{2,1,0:T(8,128)(2,1)S(1)} async-done(((bf16[8,256,512]{2,1,0:T(8,128)(2,1)}), bf16[8,256,512]{2,1,0:T(8,128)(2,1)S(1)}, u32[]{:S(2)}, u32[]{:S(2)}) %all-to-all-start.1) | async-done | bytes 2097184 | tf_op jit(solution)/shard_map/all_to_all | solution.py:354
  76.5 5.9 all-to-all-start.2
  82.8 25.2 %all-to-all-done.2 = bf16[8,32,3456]{2,1,0:T(8,128)(2,1)} async-done(((bf16[8,32,3456]{2,1,0:T(8,128)(2,1)}), bf16[8,32,3456]{2,1,0:T(8,128)(2,1)}, u32[]{:S(2)}, u32[]{:S(2)}) %all-to-all-start.2) | async-done | bytes 1769504 | tf_op jit(solution)/shard_map/all_to_all | solution.py:359
  131.3 49.8 %all-to-all-done.3 = bf16[16,64,2176]{2,1,0:T(8,128)(2,1)} async-done(((bf16[16,64,2176]{2,1,0:T(8,128)(2,1)}), bf16[16,64,2176]{2,1,0:T(8,128)(2,1)}, u32[]{:S(2)}, u32[]{:S(2)}) %all-to-all-start.3) | async-done | bytes 4456480 | tf_op jit(solution)/shard_map/all_to_all | solution.py:233
  181.1 13.3 %all_to_all.66 = bf16[8,128,128]{2,1,0:T(8,128)(2,1)S(1)} all-to-all(bf16[8,128,128]{2,1,0:T(8,128)(2,1)S(1)} %bitcast.178), channel_id=1, replica_groups=mesh['dp'=8,'z_hi'=2,'ring'=4,'tensor'=2] {'z_hi','ring'}, dimensions={0} | all-to-all | bytes 524288 | tf_op jit(solution)/shard_map/all_to_all | solution.py:408
  200.5 8.0 %collective-permute-done.1 = bf16[64,2048]{1,0:T(8,128)(2,1)S(1)} collective-permute-done((bf16[64,2048]{1,0:T(8,128)(2,1)S(1)}, bf16[64,2048]{1,0:T(8,128)(2,1)S(1)}, u32[]{:S(2)}, u32[]{:S(2)}) %collective-permute-start.1) | collective-permute-done | bytes 262176 | tf_op jit(solution)/shard_map/ppermute | solution.py:65
  218.2 56.0 %all-to-all-done.5 = bf16[16,64,2048]{2,1,0:T(8,128)(2,1)} async-done(((bf16[16,64,2048]{2,1,0:T(8,128)(2,1)}), bf16[16,64,2048]{2,1,0:T(8,128)(2,1)}, u32[]{:S(2)}, u32[]{:S(2)}) %all-to-all-start.5) | async-done | bytes 4194336 | tf_op jit(solution)/shard_map/all_to_all | solution.py:233
  274.2 26.6 %shard_map.255 = (bf16[1024,2304]{1,0:T(8,128)(2,1)}, bf16[1024,1152]{1,0:T(8,128)(2,1)}, f32[1024,128]{1,0:T(8,128)}, f32[1024,128]{1,0:T(8,128)}) custom-call(s32[1]{0:T(128)} %bitcast.31.expert_ref, bf16[1024,2048]{1,0:T(8,128)(2,1)} %bitcast.32.h_ref, bf16[1024,2176]{1,0:T(8,128)(2,1)} %bitcast.29.dy_ref, ...), custom_call_target="tpu_custom_call" | custom-call | tf_op jit(solution)/shard_map/pallas_call | solution.py:137
  300.8 6.6 %fusion.15 = bf16[1024,1024]{1,0:T(8,128)(2,1)} fusion(bf16[1024,1152]{1,0:T(8,128)(2,1)} %get-tuple-element.62.act_ref, bf16[2048,3456]{1,0:T(8,128)(2,1)} %all-gather.8.cloned.1.call-done.up_ref.down_ref), kind=kOutput, calls=%fused_computation.26 | convolution fusion | flops 2416967680 | bytes 6815744 | tf_op jit(solution)/shard_map/dot_general | solution.py:32
  312.1 13.9 %fusion.8 = bf16[1024,2048]{1,0:T(8,128)(2,1)S(1)} fusion(bf16[1024,2304]{1,0:T(8,128)(2,1)} %get-tuple-element.61.middle_ref, bf16[2048,3456]{1,0:T(8,128)(2,1)} %all-gather.8.cloned.1.call-done.up_ref.down_ref), kind=kOutput, calls=%fused_computation.20 | convolution fusion | flops 9665773568 | bytes 18350080 | tf_op jit(solution)/shard_map/dot_general | solution.py:32
  328.5 13.8 %all-to-all-done.6 = bf16[16,64,1024]{2,1,0:T(8,128)(2,1)} async-done(((bf16[16,64,1024]{2,1,0:T(8,128)(2,1)}), bf16[16,64,1024]{2,1,0:T(8,128)(2,1)}, u32[]{:S(2)}, u32[]{:S(2)}) %all-to-all-start.6) | async-done | bytes 2097184 | tf_op jit(solution)/shard_map/all_to_all | solution.py:239
  347.1 26.9 %shard_map.256 = (bf16[2048,3456]{1,0:T(8,128)(2,1)}, bf16[1024,2048]{1,0:T(8,128)(2,1)}) custom-call(bf16[1024,2048]{1,0:T(8,128)(2,1)} %bitcast.32.h_ref, bf16[1024,2176]{1,0:T(8,128)(2,1)} %bitcast.29.dy_ref, bf16[1024,2304]{1,0:T(8,128)(2,1)} %get-tuple-element.61.middle_ref, bf16[1024,1152]{1,0:T(8,128)(2,1)} %get-tuple-element.62.act_ref, ...), custom_call_target="tpu_custom_call" | custom-call | tf_op jit(solution)/shard_map/pallas_call | solution.py:178
  374.0 30.1 %all-to-all-done.7 = bf16[16,64,2176]{2,1,0:T(8,128)(2,1)} async-done(((bf16[16,64,2176]{2,1,0:T(8,128)(2,1)}), bf16[16,64,2176]{2,1,0:T(8,128)(2,1)}, u32[]{:S(2)}, u32[]{:S(2)}) %all-to-all-start.7) | async-done | bytes 4456480 | tf_op jit(solution)/shard_map/all_to_all | solution.py:239
  453.1 5.9 fusion.5
  459.0 7.2 %all-to-all-done.9 = bf16[16,64,1024]{2,1,0:T(8,128)(2,1)} async-done(((bf16[16,64,1024]{2,1,0:T(8,128)(2,1)}), bf16[16,64,1024]{2,1,0:T(8,128)(2,1)}, u32[]{:S(2)}, u32[]{:S(2)}) %all-to-all-start.9) | async-done | bytes 2097184 | tf_op jit(solution)/shard_map/all_to_all | solution.py:239
  480.6 9.7 %shard_map.257 = bf16[2048,1536]{1,0:T(8,128)(2,1)} custom-call(bf16[1024,2048]{1,0:T(8,128)(2,1)} %copy-done, bf16[1024,384]{1,0:T(8,128)(2,1)} %copy-done.4, f32[128,2048]{1,0:T(8,128)} %select_maximum_fusion.small_ref, bf16[128,2048]{1,0:T(8,128)(2,1)} %pad_maximum_fusion.3.dx_ref, bf16[128,1024]{1,0:T(8,128)(2,1)} %copy_bitcast_fusion.2.heads_ref), custom_call_target="tpu_custom_call" | custom-call | tf_op jit(solution)/shard_map/pallas_call | solution.py:213
  490.4 16.2 %collective-permute-done.3 = bf16[64,2048]{1,0:T(8,128)(2,1)S(1)} collective-permute-done((bf16[64,2048]{1,0:T(8,128)(2,1)S(1)}, bf16[64,2048]{1,0:T(8,128)(2,1)S(1)}, u32[]{:S(2)}, u32[]{:S(2)}) %collective-permute-start.3) | collective-permute-done | bytes 262176 | tf_op jit(solution)/shard_map/ppermute | solution.py:65
  507.5 14.2 %all-to-all-done.10 = bf16[16,64,2048]{2,1,0:T(8,128)(2,1)} async-done(((bf16[16,64,2048]{2,1,0:T(8,128)(2,1)}), bf16[16,64,2048]{2,1,0:T(8,128)(2,1)}, u32[]{:S(2)}, u32[]{:S(2)}) %all-to-all-start.10) | async-done | bytes 4194336 | tf_op jit(solution)/shard_map/all_to_all | solution.py:239
  521.7 6.2 %all-to-all-start.11 = ((bf16[8,32,3456]{2,1,0:T(8,128)(2,1)}), bf16[8,32,3456]{2,1,0:T(8,128)(2,1)S(1)}, u32[]{:S(2)}, u32[]{:S(2)}) async-start(bf16[8,32,3456]{2,1,0:T(8,128)(2,1)} %bitcast.165), calls=%async_computation.12 | async-start | bytes 3538944 | tf_op jit(solution)/shard_map/all_to_all | solution.py:498
  532.0 25.8 %collective-permute-done.4 = f32[64,2048]{1,0:T(8,128)S(1)} collective-permute-done((f32[64,2048]{1,0:T(8,128)S(1)}, f32[64,2048]{1,0:T(8,128)S(1)}, u32[]{:S(2)}, u32[]{:S(2)}) %collective-permute-start.4) | collective-permute-done | bytes 524320 | tf_op jit(solution)/shard_map/ppermute | solution.py:65
  564.0 6.8 %all-to-all-start.12 = ((bf16[8,32,1536]{2,1,0:T(8,128)(2,1)}), bf16[8,32,1536]{2,1,0:T(8,128)(2,1)S(1)}, u32[]{:S(2)}, u32[]{:S(2)}) async-start(bf16[8,32,1536]{2,1,0:T(8,128)(2,1)} %bitcast.171), calls=%async_computation.14 | async-start | bytes 1572864 | tf_op jit(solution)/shard_map/all_to_all | solution.py:501
  577.9 8.3 %all-to-all-done.12 = bf16[8,32,1536]{2,1,0:T(8,128)(2,1)S(1)} async-done(((bf16[8,32,1536]{2,1,0:T(8,128)(2,1)}), bf16[8,32,1536]{2,1,0:T(8,128)(2,1)S(1)}, u32[]{:S(2)}, u32[]{:S(2)}) %all-to-all-start.12) | async-done | bytes 786464 | tf_op jit(solution)/shard_map/all_to_all | solution.py:501
  (263 shorter events, 169.5 us)
Async XLA Ops:
  7.2 68.2 %all-gather.4.cloned.1.call-start = ((), (), s32[]{:S(2)}) async-start(), calls=%async_computation.15 | async-start | bytes 5242880 | tf_op jit(solution)/shard_map/all_gather | solution.py:349
  7.3 16.3 %collective-permute-start = (bf16[128,2048]{1,0:T(8,128)(2,1)}, bf16[128,2048]{1,0:T(8,128)(2,1)S(1)}, u32[]{:S(2)}, u32[]{:S(2)}) collective-permute-start(bf16[128,2048]{1,0:T(8,128)(2,1)} %bitcast.161), channel_id=1, source_target_pairs={{0,9},{1,8},{2,11},{3,10},{4,13},{5,12},{6,15},{7,14},{8,1},{9,0},... | collective-permute-start | bytes 1572872 | tf_op jit(solution)/shard_map/ppermute | solution.py:61
  42.4 28.8 %all-to-all-start.1 = ((bf16[8,256,512]{2,1,0:T(8,128)(2,1)}), bf16[8,256,512]{2,1,0:T(8,128)(2,1)S(1)}, u32[]{:S(2)}, u32[]{:S(2)}) async-start(bf16[8,256,512]{2,1,0:T(8,128)(2,1)} %broadcast_in_dim.116), calls=%async_computation.1 | async-start | bytes 4194304 | tf_op jit(solution)/shard_map/all_to_all | solution.py:354
  47.2 149.0 %all-gather.6.cloned.1.call-start = ((), (), s32[]{:S(2)}) async-start(), calls=%async_computation.16 | async-start | bytes 4259840 | tf_op jit(solution)/shard_map/all_gather | solution.py:356
  54.8 27.9 %copy-start.18 = (bf16[1,128,2048]{2,1,0:T(8,128)(2,1)S(1)}, bf16[1,128,2048]{2,1,0:T(8,128)(2,1)}, u32[]{:S(2)}) copy-start(bf16[1,128,2048]{2,1,0:T(8,128)(2,1)} %param.17) | copy-start | bytes 1572868
  76.5 31.6 %all-to-all-start.2 = ((bf16[8,32,3456]{2,1,0:T(8,128)(2,1)}), bf16[8,32,3456]{2,1,0:T(8,128)(2,1)}, u32[]{:S(2)}, u32[]{:S(2)}) async-start(bf16[8,32,3456]{2,1,0:T(8,128)(2,1)} %pad_dynamic-update-slice_fusion.1), calls=%async_computation.2 | async-start | bytes 3538944 | tf_op jit(solution)/shard_map/all_to_all | solution.py:359
  110.7 70.5 %all-to-all-start.3 = ((bf16[16,64,2176]{2,1,0:T(8,128)(2,1)}), bf16[16,64,2176]{2,1,0:T(8,128)(2,1)}, u32[]{:S(2)}, u32[]{:S(2)}) async-start(bf16[16,64,2176]{2,1,0:T(8,128)(2,1)} %broadcast_in_dim.121), calls=%async_computation.3 | async-start | bytes 8912896 | tf_op jit(solution)/shard_map/all_to_all | solution.py:233
  115.2 159.0 %all-gather.8.cloned.1.call-start = ((), (), s32[]{:S(2)}) async-start(), calls=%async_computation.17 | async-start | bytes 15925248 | tf_op jit(solution)/shard_map/all_gather | solution.py:410
  131.3 77.2 %copy-start.7 = (bf16[1,128,2048]{2,1,0:T(8,128)(2,1)S(1)}, bf16[1,128,2048]{2,1,0:T(8,128)(2,1)}, u32[]{:S(2)}) copy-start(bf16[1,128,2048]{2,1,0:T(8,128)(2,1)} %param.16) | copy-start | bytes 1572868
  200.0 8.5 %collective-permute-start.1 = (bf16[64,2048]{1,0:T(8,128)(2,1)S(1)}, bf16[64,2048]{1,0:T(8,128)(2,1)S(1)}, u32[]{:S(2)}, u32[]{:S(2)}) collective-permute-start(bf16[64,2048]{1,0:T(8,128)(2,1)S(1)} %dynamic-slice_convert_fusion), channel_id=1, source_target_pairs={{0,1},{1,0},{2,3},{3,2},{4,5},{5,4},{6,7},{7,6},{8,9},{9,8},{10,11... | collective-permute-start | bytes 786440 | tf_op jit(solution)/shard_map/ppermute | solution.py:65
  212.2 62.0 %all-to-all-start.5 = ((bf16[16,64,2048]{2,1,0:T(8,128)(2,1)}), bf16[16,64,2048]{2,1,0:T(8,128)(2,1)}, u32[]{:S(2)}, u32[]{:S(2)}) async-start(bf16[16,64,2048]{2,1,0:T(8,128)(2,1)} %broadcast_in_dim.122), calls=%async_computation.5 | async-start | bytes 8388608 | tf_op jit(solution)/shard_map/all_to_all | solution.py:233
  307.5 34.8 %all-to-all-start.6 = ((bf16[16,64,1024]{2,1,0:T(8,128)(2,1)}), bf16[16,64,1024]{2,1,0:T(8,128)(2,1)}, u32[]{:S(2)}, u32[]{:S(2)}) async-start(bf16[16,64,1024]{2,1,0:T(8,128)(2,1)} %bitcast.164), calls=%async_computation.6 | async-start | bytes 4194304 | tf_op jit(solution)/shard_map/all_to_all | solution.py:239
  342.2 61.8 %all-to-all-start.7 = ((bf16[16,64,2176]{2,1,0:T(8,128)(2,1)}), bf16[16,64,2176]{2,1,0:T(8,128)(2,1)}, u32[]{:S(2)}, u32[]{:S(2)}) async-start(bf16[16,64,2176]{2,1,0:T(8,128)(2,1)} %bitcast.149), calls=%async_computation.7 | async-start | bytes 8912896 | tf_op jit(solution)/shard_map/all_to_all | solution.py:239
  347.0 174.7 %reduce-scatter.3.cloned.1.call-start = ((), (), s32[]{:S(2)}) async-start(), calls=%async_computation.18 | async-start | bytes 15925248 | tf_op jit(solution)/shard_map/reduce_scatter | solution.py:437
  412.4 6.5 %collective-permute-start.2 = (bf16[64,2048]{1,0:T(8,128)(2,1)S(1)}, bf16[64,2048]{1,0:T(8,128)(2,1)S(1)}, u32[]{:S(2)}, u32[]{:S(2)}) collective-permute-start(bf16[64,2048]{1,0:T(8,128)(2,1)S(1)} %fusion.81), channel_id=1, source_target_pairs={{0,1},{1,0},{2,3},{3,2},{4,5},{5,4},{6,7},{7,6},{8,9},{9,8},{10,11... | collective-permute-start | bytes 786440 | tf_op jit(solution)/shard_map/ppermute | solution.py:65
  423.3 12.1 %all-to-all-start.8 = ((bf16[8,128,128]{2,1,0:T(8,128)(2,1)}), bf16[8,128,128]{2,1,0:T(8,128)(2,1)S(1)}, u32[]{:S(2)}, u32[]{:S(2)}) async-start(bf16[8,128,128]{2,1,0:T(8,128)(2,1)} %bitcast.145), calls=%async_computation.8 | async-start | bytes 524288 | tf_op jit(solution)/shard_map/all_to_all | solution.py:459
  435.5 30.7 %all-to-all-start.9 = ((bf16[16,64,1024]{2,1,0:T(8,128)(2,1)}), bf16[16,64,1024]{2,1,0:T(8,128)(2,1)}, u32[]{:S(2)}, u32[]{:S(2)}) async-start(bf16[16,64,1024]{2,1,0:T(8,128)(2,1)} %bitcast.159), calls=%async_computation.9 | async-start | bytes 4194304 | tf_op jit(solution)/shard_map/all_to_all | solution.py:239
  466.2 55.5 %all-to-all-start.10 = ((bf16[16,64,2048]{2,1,0:T(8,128)(2,1)}), bf16[16,64,2048]{2,1,0:T(8,128)(2,1)}, u32[]{:S(2)}, u32[]{:S(2)}) async-start(bf16[16,64,2048]{2,1,0:T(8,128)(2,1)} %bitcast.160), calls=%async_computation.10 | async-start | bytes 8388608 | tf_op jit(solution)/shard_map/all_to_all | solution.py:239
  471.1 91.7 %reduce-scatter.5.cloned.1.call-start = ((), (), s32[]{:S(2)}) async-start(), calls=%async_computation.19 | async-start | bytes 7077888 | tf_op jit(solution)/shard_map/reduce_scatter | solution.py:488
  477.1 29.5 %collective-permute-start.3 = (bf16[64,2048]{1,0:T(8,128)(2,1)S(1)}, bf16[64,2048]{1,0:T(8,128)(2,1)S(1)}, u32[]{:S(2)}, u32[]{:S(2)}) collective-permute-start(bf16[64,2048]{1,0:T(8,128)(2,1)S(1)} %fusion.64), channel_id=1, source_target_pairs={{0,1},{1,0},{2,3},{3,2},{4,5},{5,4},{6,7},{7,6},{8,9},{9,8},{10,11... | collective-permute-start | bytes 786440 | tf_op jit(solution)/shard_map/ppermute | solution.py:65
  521.7 37.2 %all-to-all-start.11 = ((bf16[8,32,3456]{2,1,0:T(8,128)(2,1)}), bf16[8,32,3456]{2,1,0:T(8,128)(2,1)S(1)}, u32[]{:S(2)}, u32[]{:S(2)}) async-start(bf16[8,32,3456]{2,1,0:T(8,128)(2,1)} %bitcast.165), calls=%async_computation.12 | async-start | bytes 3538944 | tf_op jit(solution)/shard_map/all_to_all | solution.py:498
  531.7 26.1 %collective-permute-start.4 = (f32[64,2048]{1,0:T(8,128)S(1)}, f32[64,2048]{1,0:T(8,128)S(1)}, u32[]{:S(2)}, u32[]{:S(2)}) collective-permute-start(f32[64,2048]{1,0:T(8,128)S(1)} %fusion.46), channel_id=1, source_target_pairs={{0,1},{1,0},{2,3},{3,2},{4,5},{5,4},{6,7},{7,6},{8,9},{9,8},{10,11... | collective-permute-start | bytes 1572872 | tf_op jit(solution)/shard_map/ppermute | solution.py:65
  564.0 22.1 %all-to-all-start.12 = ((bf16[8,32,1536]{2,1,0:T(8,128)(2,1)}), bf16[8,32,1536]{2,1,0:T(8,128)(2,1)S(1)}, u32[]{:S(2)}, u32[]{:S(2)}) async-start(bf16[8,32,1536]{2,1,0:T(8,128)(2,1)} %bitcast.171), calls=%async_computation.14 | async-start | bytes 1572864 | tf_op jit(solution)/shard_map/all_to_all | solution.py:501
  586.3 3.8 collective-permute-start.5
  (38 other events, 337.3 us)
Sparse Core Ops, SparseCore 0:
  25.9 49.5 all-gather.3
  78.7 117.4 all-gather.5
  197.9 72.2 all-gather.7
  404.2 74.7 reduce-scatter.2
  521.8 40.9 reduce-scatter.4

commit v3 on v2

--- a/solution.py
+++ b/solution.py
@@ -319,6 +319,7 @@
             jnp.broadcast_to(misc[None], (heads, depth, n_misc)),
             bias_rows[:, :, None],
             jnp.zeros((heads, depth, LANES - n_misc - 1), BF),
+            jnp.broadcast_to(w_proj.T[None], (heads, depth, heads * HD)),
         ],
         axis=2,
     )
@@ -349,16 +350,16 @@
     x_all = lax.all_gather(both_rings(hidden_in[0]), "ring", axis=1, tiled=True)
     x_all = x_all.reshape(length, width)
 
-    attn_blob = lax.all_to_all(attn_blob, SEQ, 0, 0, tiled=True).reshape(1, seqs * depth, -1)
-    attn_full = jnp.broadcast_to(attn_blob, (dps, *attn_blob.shape[1:]))
+    attn_blob = lax.all_to_all(attn_blob, SEQ, 0, 0, tiled=True).reshape(seqs * depth, -1)
+    attn_cols = 3 * HD + LANES
+    proj_rows = attn_blob[:, attn_cols:]
+    attn_full = jnp.broadcast_to(attn_blob[None, :, :attn_cols], (dps, seqs * depth, attn_cols))
     attn_full = lax.all_to_all(attn_full, "dp", 0, 0, tiled=True).reshape(width, -1)
-    x_all, attn_full, proj_rows, ffn_blob = together(x_all, attn_full, w_proj.T, ffn_blob)
-    proj_rows = lax.all_gather(proj_rows, ("dp", *SEQ), axis=0, tiled=True)
+    x_all, attn_full, proj_rows, ffn_blob = together(x_all, attn_full, proj_rows, ffn_blob)
+    proj_rows = lax.all_gather(proj_rows, "dp", axis=0, tiled=True)
     qkv_full = attn_full[:, : 3 * HD]
     misc_full = attn_full[:, 3 * HD :]
     ffn_blob = lax.all_to_all(ffn_blob, SEQ, 0, 0, tiled=True)
-    ffn_blob, dy_slots = together(ffn_blob, jnp.concatenate([dy_own, slot_cols], 1))
-    dy_slots = plane_gather(dy_slots)
 
     bias_full = misc_full[:, n_misc].reshape(dps * seqs, depth)[:, : 3 * bias_part]
     bias_full = bias_full.reshape(dps * seqs, 3, bias_part).transpose(1, 0, 2).reshape(1, 3 * HD)
@@ -404,9 +405,11 @@
     probs_low = attn_probs.astype(BF)
     attn_head = mm(probs_low, value).astype(BF)
 
-    by_head, dy_slots = together(attn_head.reshape(seqs, rows, HD), dy_slots)
+    by_head, ffn_blob = together(attn_head.reshape(seqs, rows, HD), ffn_blob)
     by_head = lax.all_to_all(by_head, SEQ, 0, 0, tiled=True)
-    by_head, ffn_blob = together(by_head, ffn_blob)
+    dy_slots = jnp.concatenate([dy_own, slot_cols], 1)
+    by_head, ffn_blob, dy_slots = together(by_head, ffn_blob, dy_slots)
+    dy_slots = plane_gather(dy_slots)
     ffn_full = lax.all_gather(ffn_blob.reshape(seqs * depth, -1), "dp", axis=0, tiled=True)
     w_up = ffn_full[:, : 2 * units]
     attn_flat = by_head.transpose(1, 0, 2).reshape(rows, heads * HD)
@@ -417,7 +420,8 @@
     scale_two = rms_scale(after_attn)
     norm_two = after_attn * scale_two
     normed_two = (norm_two * gain_ffn).astype(BF)
-    h_all = plane_gather(normed_two)
+    normed_sent, dy_slots = together(normed_two, dy_slots)
+    h_all = plane_gather(normed_sent)
 
     expert = me_seq.astype(jnp.int32).reshape(1)
     dgate_up, act_weighed, dots, router = feed_forward(

time: 604 us -> 593 us (0.982)
  waiting for transfers between devices: 299 us -> 284 us
  blocking collectives: 27.4 us -> 20.9 us
    all_to_all x2, waiting for transfers between devices: 106 us -> 78.7 us  [plane_gather(): lax.all_to_all(copies, GRID, 0, 0, tiled=True).reshape(count * n, width)]
    ppermute x5, waiting for transfers between devices: 56 us -> 73.5 us  [swap(): return lax.ppermute(x, 'tensor', [(0, 1), (1, 0)])]
    all_to_all x1, waiting for transfers between devices: 25.2 us -> 9.75 us  [body(): ffn_blob = lax.all_to_all(ffn_blob, SEQ, 0, 0, tiled=True)]
    all_to_all x0 -> x1, waiting for transfers between devices: none -> 8.71 us  [body(): by_head = lax.all_to_all(by_head, SEQ, 0, 0, tiled=True)]
    reduce_scatter x1, waiting for transfers between devices: 3.88 us -> 10.6 us  [body(): lax.psum_scatter(attn_grad, 'dp', scatter_dimension=0, tiled=True)]
    all_to_all x2 -> x1, blocking collectives: 27.4 us -> 20.9 us  [body(): lax.all_to_all(attn_blob, SEQ, 0, 0, tiled=True).reshape(seqs * depth, -1)]
  transfers between devices with their start and end apart: 22 -> 23, of which waited for: 19 -> 18; matrix products, arithmetic and copies ran while one was open for 19% -> 20% of each run, Pallas kernels for 6% -> 6%
where the time goes in v3:
time: 593 us; the launch traced here: 587 us
  waiting for transfers between devices  284 us (48%)
  starting transfers between devices  69.1 us (12%)
  Pallas kernels  63.4 us (11%)
  local copies, waits for them, and re-layouts  47.8 us (8%)
  matrix products  46.5 us (8%)
  other arithmetic  39.4 us (7%)
  blocking collectives  20.9 us (4%)
  between operations  15.3 us (3%)
    all_to_all x2, waiting for transfers between devices, plane_gather(): lax.all_to_all(copies, GRID, 0, 0, tiled=True).reshape(count * n, width)  78.7 us
    ppermute x5, waiting for transfers between devices, swap(): return lax.ppermute(x, 'tensor', [(0, 1), (1, 0)])  73.5 us
    all_to_all x4, waiting for transfers between devices, send_parts(): return lax.all_to_all(parts, GRID, 0, 0, tiled=True)  68.4 us
    dot_general x14, matrix products, dot(): return lax.dot_general(a, b, (dims, ((), ())), preferred_element_type=F32)  46.5 us
    pallas_call x1, Pallas kernels, ffn_rest(): pl.pallas_call(ffn_rest_kernel, grid=(width // step,), in_specs=[pl.Block...  26.9 us
    pallas_call x1, Pallas kernels, feed_forward(): pl.pallas_call(functools.partial(feed_forward_kernel, capacity), grid_spe...  26.6 us
    all_to_all x1, blocking collectives, body(): lax.all_to_all(attn_blob, SEQ, 0, 0, tiled=True).reshape(seqs * depth, -1)  20.9 us
    all_to_all x4, starting transfers between devices, send_parts(): return lax.all_to_all(parts, GRID, 0, 0, tiled=True)  18.8 us
  transfers between devices with their start and end apart: 23, of which 18 were waited for; matrix products, arithmetic and copies ran while one was open for 20% of the time, Pallas kernels for 6%

profile of v3, /device:TPU:4, one launch (start us, length us, event | category | flops | bytes accessed | tf_op | source)
XLA Modules:
  0.0 586.5 jit_solution(6357392515925847776)
XLA Ops:
  11.4 12.1 %collective-permute-done = bf16[128,2048]{1,0:T(8,128)(2,1)S(1)} collective-permute-done((bf16[128,2048]{1,0:T(8,128)(2,1)}, bf16[128,2048]{1,0:T(8,128)(2,1)S(1)}, u32[]{:S(2)}, u32[]{:S(2)}) %collective-permute-start) | collective-permute-done | bytes 524320 | tf_op jit(solution)/shard_map/ppermute | solution.py:61
  27.1 20.9 %all_to_all.65 = bf16[8,32,1536]{2,1,0:T(8,128)(2,1)S(1)} all-to-all(bf16[8,32,1536]{2,1,0:T(8,128)(2,1)S(1)} %concatenate.77), channel_id=1, replica_groups=mesh['dp'=8,'z_hi'=2,'ring'=4,'tensor'=2] {'z_hi','ring'}, dimensions={0} | all-to-all | bytes 1572864 | tf_op jit(solution)/shard_map/all_to_all | solution.py:353
  70.0 8.3 %all-to-all-done.1 = bf16[8,256,512]{2,1,0:T(8,128)(2,1)S(1)} async-done(((bf16[8,256,512]{2,1,0:T(8,128)(2,1)}), bf16[8,256,512]{2,1,0:T(8,128)(2,1)S(1)}, u32[]{:S(2)}, u32[]{:S(2)}) %all-to-all-start.1) | async-done | bytes 2097184 | tf_op jit(solution)/shard_map/all_to_all | solution.py:357
  102.0 9.7 %all-to-all-done.2 = bf16[8,32,3456]{2,1,0:T(8,128)(2,1)} async-done(((bf16[8,32,3456]{2,1,0:T(8,128)(2,1)}), bf16[8,32,3456]{2,1,0:T(8,128)(2,1)}, u32[]{:S(2)}, u32[]{:S(2)}) %all-to-all-start.2) | async-done | bytes 1769504 | tf_op jit(solution)/shard_map/all_to_all | solution.py:362
  116.6 8.7 %all-to-all-done.3 = bf16[8,128,128]{2,1,0:T(8,128)(2,1)S(1)} async-done(((bf16[8,128,128]{2,1,0:T(8,128)(2,1)}), bf16[8,128,128]{2,1,0:T(8,128)(2,1)S(1)}, u32[]{:S(2)}, u32[]{:S(2)}) %all-to-all-start.3) | async-done | bytes 262176 | tf_op jit(solution)/shard_map/all_to_all | solution.py:409
  128.0 6.7 %all-to-all-start.4 = ((bf16[16,64,2176]{2,1,0:T(8,128)(2,1)}), bf16[16,64,2176]{2,1,0:T(8,128)(2,1)}, u32[]{:S(2)}, u32[]{:S(2)}) async-start(bf16[16,64,2176]{2,1,0:T(8,128)(2,1)} %broadcast_in_dim.126), calls=%async_computation.4 | async-start | bytes 8912896 | tf_op jit(solution)/shard_map/all_to_all | solution.py:233
  141.7 27.8 %collective-permute-done.1 = bf16[64,2048]{1,0:T(8,128)(2,1)S(1)} collective-permute-done((bf16[64,2048]{1,0:T(8,128)(2,1)S(1)}, bf16[64,2048]{1,0:T(8,128)(2,1)S(1)}, u32[]{:S(2)}, u32[]{:S(2)}) %collective-permute-start.1) | collective-permute-done | bytes 262176 | tf_op jit(solution)/shard_map/ppermute | solution.py:65
  169.8 22.6 %all-to-all-done.4 = bf16[16,64,2176]{2,1,0:T(8,128)(2,1)} async-done(((bf16[16,64,2176]{2,1,0:T(8,128)(2,1)}), bf16[16,64,2176]{2,1,0:T(8,128)(2,1)}, u32[]{:S(2)}, u32[]{:S(2)}) %all-to-all-start.4) | async-done | bytes 4456480 | tf_op jit(solution)/shard_map/all_to_all | solution.py:233
  200.6 56.2 %all-to-all-done.5 = bf16[16,64,2048]{2,1,0:T(8,128)(2,1)} async-done(((bf16[16,64,2048]{2,1,0:T(8,128)(2,1)}), bf16[16,64,2048]{2,1,0:T(8,128)(2,1)}, u32[]{:S(2)}, u32[]{:S(2)}) %all-to-all-start.5) | async-done | bytes 4194336 | tf_op jit(solution)/shard_map/all_to_all | solution.py:233
  256.7 26.6 %shard_map.255 = (bf16[1024,2304]{1,0:T(8,128)(2,1)}, bf16[1024,1152]{1,0:T(8,128)(2,1)}, f32[1024,128]{1,0:T(8,128)}, f32[1024,128]{1,0:T(8,128)}) custom-call(s32[1]{0:T(128)} %bitcast.30.expert_ref, bf16[1024,2048]{1,0:T(8,128)(2,1)} %bitcast.32.h_ref, bf16[1024,2176]{1,0:T(8,128)(2,1)} %bitcast.31.dy_ref, ...), custom_call_target="tpu_custom_call" | custom-call | tf_op jit(solution)/shard_map/pallas_call | solution.py:137
  283.3 6.7 %fusion.15 = bf16[1024,1024]{1,0:T(8,128)(2,1)} fusion(bf16[1024,1152]{1,0:T(8,128)(2,1)} %get-tuple-element.64.act_ref, bf16[2048,3456]{1,0:T(8,128)(2,1)} %all-gather.8.cloned.1.call-done.up_ref.down_ref), kind=kOutput, calls=%fused_computation.26 | convolution fusion | flops 2416967680 | bytes 6815744 | tf_op jit(solution)/shard_map/dot_general | solution.py:32
  294.6 13.9 %fusion.8 = bf16[1024,2048]{1,0:T(8,128)(2,1)S(1)} fusion(bf16[1024,2304]{1,0:T(8,128)(2,1)} %get-tuple-element.63.middle_ref, bf16[2048,3456]{1,0:T(8,128)(2,1)} %all-gather.8.cloned.1.call-done.up_ref.down_ref), kind=kOutput, calls=%fused_computation.20 | convolution fusion | flops 9665773568 | bytes 18350080 | tf_op jit(solution)/shard_map/dot_general | solution.py:32
  311.0 13.1 %all-to-all-done.6 = bf16[16,64,1024]{2,1,0:T(8,128)(2,1)} async-done(((bf16[16,64,1024]{2,1,0:T(8,128)(2,1)}), bf16[16,64,1024]{2,1,0:T(8,128)(2,1)}, u32[]{:S(2)}, u32[]{:S(2)}) %all-to-all-start.6) | async-done | bytes 2097184 | tf_op jit(solution)/shard_map/all_to_all | solution.py:239
  329.0 26.9 %shard_map.256 = (bf16[2048,3456]{1,0:T(8,128)(2,1)}, bf16[1024,2048]{1,0:T(8,128)(2,1)}) custom-call(bf16[1024,2048]{1,0:T(8,128)(2,1)} %bitcast.32.h_ref, bf16[1024,2176]{1,0:T(8,128)(2,1)} %bitcast.31.dy_ref, bf16[1024,2304]{1,0:T(8,128)(2,1)} %get-tuple-element.63.middle_ref, bf16[1024,1152]{1,0:T(8,128)(2,1)} %get-tuple-element.64.act_ref, ...), custom_call_target="tpu_custom_call" | custom-call | tf_op jit(solution)/shard_map/pallas_call | solution.py:178
  355.9 28.8 %all-to-all-done.7 = bf16[16,64,2176]{2,1,0:T(8,128)(2,1)} async-done(((bf16[16,64,2176]{2,1,0:T(8,128)(2,1)}), bf16[16,64,2176]{2,1,0:T(8,128)(2,1)}, u32[]{:S(2)}, u32[]{:S(2)}) %all-to-all-start.7) | async-done | bytes 4456480 | tf_op jit(solution)/shard_map/all_to_all | solution.py:239
  433.7 5.9 %fusion.5 = (f32[2048]{0:T(1024)S(1)}, bf16[1024,2048]{1,0:T(8,128)(2,1)}) fusion(bf16[1024,2048]{1,0:T(8,128)(2,1)} %bitcast.151, f32[1024]{0:T(1024)S(1)} %add_rsqrt_fusion, bf16[1024,384]{1,0:T(8,128)(2,1)S(1)} %concatenate.85.linear_ref, bf16[2048,512]{1,0:T(8,128)(2,1)S(1)} %bitcast.158), kind=kOutput, calls=%fused_computation.8 | convolution fusion | flops 1621096448 | bytes 10760192 | tf_op jit(solution)/shard_map/dot_general | solution.py:32
  439.6 6.4 %all-to-all-done.9 = bf16[16,64,1024]{2,1,0:T(8,128)(2,1)} async-done(((bf16[16,64,1024]{2,1,0:T(8,128)(2,1)}), bf16[16,64,1024]{2,1,0:T(8,128)(2,1)}, u32[]{:S(2)}, u32[]{:S(2)}) %all-to-all-start.9) | async-done | bytes 2097184 | tf_op jit(solution)/shard_map/all_to_all | solution.py:239
  460.5 9.9 %shard_map.257 = bf16[2048,1536]{1,0:T(8,128)(2,1)} custom-call(bf16[1024,2048]{1,0:T(8,128)(2,1)} %copy-done, bf16[1024,384]{1,0:T(8,128)(2,1)} %copy-done.4, f32[128,2048]{1,0:T(8,128)} %select_maximum_fusion.small_ref, bf16[128,2048]{1,0:T(8,128)(2,1)} %pad_maximum_fusion.3.dx_ref, bf16[128,1024]{1,0:T(8,128)(2,1)} %copy_bitcast_fusion.2.heads_ref), custom_call_target="tpu_custom_call" | custom-call | tf_op jit(solution)/shard_map/pallas_call | solution.py:213
  470.4 13.7 %collective-permute-done.3 = bf16[64,2048]{1,0:T(8,128)(2,1)S(1)} collective-permute-done((bf16[64,2048]{1,0:T(8,128)(2,1)S(1)}, bf16[64,2048]{1,0:T(8,128)(2,1)S(1)}, u32[]{:S(2)}, u32[]{:S(2)}) %collective-permute-start.3) | collective-permute-done | bytes 262176 | tf_op jit(solution)/shard_map/ppermute | solution.py:65
  485.0 20.1 %all-to-all-done.10 = bf16[16,64,2048]{2,1,0:T(8,128)(2,1)} async-done(((bf16[16,64,2048]{2,1,0:T(8,128)(2,1)}), bf16[16,64,2048]{2,1,0:T(8,128)(2,1)}, u32[]{:S(2)}, u32[]{:S(2)}) %all-to-all-start.10) | async-done | bytes 4194336 | tf_op jit(solution)/shard_map/all_to_all | solution.py:239
  513.2 25.8 %collective-permute-done.4 = f32[64,2048]{1,0:T(8,128)S(1)} collective-permute-done((f32[64,2048]{1,0:T(8,128)S(1)}, f32[64,2048]{1,0:T(8,128)S(1)}, u32[]{:S(2)}, u32[]{:S(2)}) %collective-permute-start.4) | collective-permute-done | bytes 524320 | tf_op jit(solution)/shard_map/ppermute | solution.py:65
  540.1 10.6 %reduce-scatter.5.cloned.1.call-done = bf16[256,1536]{1,0:T(8,128)(2,1)} async-done(((bf16[2048,1536]{1,0:T(8,128)(2,1)}), bf16[256,1536]{1,0:T(8,128)(2,1)}) %reduce-scatter.5.cloned.1.call-update) | async-done | bytes 786448 | tf_op jit(solution)/shard_map/reduce_scatter | solution.py:492
  551.9 6.8 %all-to-all-start.12 = ((bf16[8,32,1536]{2,1,0:T(8,128)(2,1)}), bf16[8,32,1536]{2,1,0:T(8,128)(2,1)S(1)}, u32[]{:S(2)}, u32[]{:S(2)}) async-start(bf16[8,32,1536]{2,1,0:T(8,128)(2,1)} %bitcast.172), calls=%async_computation.14 | async-start | bytes 1572864 | tf_op jit(solution)/shard_map/all_to_all | solution.py:505
  565.8 8.3 %all-to-all-done.12 = bf16[8,32,1536]{2,1,0:T(8,128)(2,1)S(1)} async-done(((bf16[8,32,1536]{2,1,0:T(8,128)(2,1)}), bf16[8,32,1536]{2,1,0:T(8,128)(2,1)S(1)}, u32[]{:S(2)}, u32[]{:S(2)}) %all-to-all-start.12) | async-done | bytes 786464 | tf_op jit(solution)/shard_map/all_to_all | solution.py:505
  (266 shorter events, 174.8 us)
Async XLA Ops:
  7.3 71.1 %all-gather.4.cloned.1.call-start = ((), (), s32[]{:S(2)}) async-start(), calls=%async_computation.15 | async-start | bytes 5242880 | tf_op jit(solution)/shard_map/all_gather | solution.py:350
  7.3 16.3 %collective-permute-start = (bf16[128,2048]{1,0:T(8,128)(2,1)}, bf16[128,2048]{1,0:T(8,128)(2,1)S(1)}, u32[]{:S(2)}, u32[]{:S(2)}) collective-permute-start(bf16[128,2048]{1,0:T(8,128)(2,1)} %bitcast.161), channel_id=1, source_target_pairs={{0,9},{1,8},{2,11},{3,10},{4,13},{5,12},{6,15},{7,14},{8,1},{9,0},... | collective-permute-start | bytes 1572872 | tf_op jit(solution)/shard_map/ppermute | solution.py:61
  49.5 28.8 %all-to-all-start.1 = ((bf16[8,256,512]{2,1,0:T(8,128)(2,1)}), bf16[8,256,512]{2,1,0:T(8,128)(2,1)S(1)}, u32[]{:S(2)}, u32[]{:S(2)}) async-start(bf16[8,256,512]{2,1,0:T(8,128)(2,1)} %broadcast_in_dim.121), calls=%async_computation.1 | async-start | bytes 4194304 | tf_op jit(solution)/shard_map/all_to_all | solution.py:357
  54.3 80.4 %all-gather.6.cloned.1.call-start = ((), (), s32[]{:S(2)}) async-start(), calls=%async_computation.16 | async-start | bytes 4718592 | tf_op jit(solution)/shard_map/all_gather | solution.py:359
  81.6 30.2 %all-to-all-start.2 = ((bf16[8,32,3456]{2,1,0:T(8,128)(2,1)}), bf16[8,32,3456]{2,1,0:T(8,128)(2,1)}, u32[]{:S(2)}, u32[]{:S(2)}) async-start(bf16[8,32,3456]{2,1,0:T(8,128)(2,1)} %pad_dynamic-update-slice_fusion.1), calls=%async_computation.2 | async-start | bytes 3538944 | tf_op jit(solution)/shard_map/all_to_all | solution.py:362
  111.7 13.6 %all-to-all-start.3 = ((bf16[8,128,128]{2,1,0:T(8,128)(2,1)}), bf16[8,128,128]{2,1,0:T(8,128)(2,1)S(1)}, u32[]{:S(2)}, u32[]{:S(2)}) async-start(bf16[8,128,128]{2,1,0:T(8,128)(2,1)} %bitcast.27), calls=%async_computation.3 | async-start | bytes 524288 | tf_op jit(solution)/shard_map/all_to_all | solution.py:409
  116.6 140.2 %all-gather.8.cloned.1.call-start = ((), (), s32[]{:S(2)}) async-start(), calls=%async_computation.17 | async-start | bytes 15925248 | tf_op jit(solution)/shard_map/all_gather | solution.py:413
  128.0 64.4 %all-to-all-start.4 = ((bf16[16,64,2176]{2,1,0:T(8,128)(2,1)}), bf16[16,64,2176]{2,1,0:T(8,128)(2,1)}, u32[]{:S(2)}, u32[]{:S(2)}) async-start(bf16[16,64,2176]{2,1,0:T(8,128)(2,1)} %broadcast_in_dim.126), calls=%async_computation.4 | async-start | bytes 8912896 | tf_op jit(solution)/shard_map/all_to_all | solution.py:233
  134.7 34.7 %copy-start.7 = (bf16[1,128,2048]{2,1,0:T(8,128)(2,1)S(1)}, bf16[1,128,2048]{2,1,0:T(8,128)(2,1)}, u32[]{:S(2)}) copy-start(bf16[1,128,2048]{2,1,0:T(8,128)(2,1)} %param.16) | copy-start | bytes 1572868
  139.1 30.3 %collective-permute-start.1 = (bf16[64,2048]{1,0:T(8,128)(2,1)S(1)}, bf16[64,2048]{1,0:T(8,128)(2,1)S(1)}, u32[]{:S(2)}, u32[]{:S(2)}) collective-permute-start(bf16[64,2048]{1,0:T(8,128)(2,1)S(1)} %dynamic-slice_convert_fusion), channel_id=1, source_target_pairs={{0,1},{1,0},{2,3},{3,2},{4,5},{5,4},{6,7},{7,6},{8,9},{9,8},{10,11... | collective-permute-start | bytes 786440 | tf_op jit(solution)/shard_map/ppermute | solution.py:65
  195.0 61.8 %all-to-all-start.5 = ((bf16[16,64,2048]{2,1,0:T(8,128)(2,1)}), bf16[16,64,2048]{2,1,0:T(8,128)(2,1)}, u32[]{:S(2)}, u32[]{:S(2)}) async-start(bf16[16,64,2048]{2,1,0:T(8,128)(2,1)} %broadcast_in_dim.127), calls=%async_computation.5 | async-start | bytes 8388608 | tf_op jit(solution)/shard_map/all_to_all | solution.py:233
  290.0 34.1 %all-to-all-start.6 = ((bf16[16,64,1024]{2,1,0:T(8,128)(2,1)}), bf16[16,64,1024]{2,1,0:T(8,128)(2,1)}, u32[]{:S(2)}, u32[]{:S(2)}) async-start(bf16[16,64,1024]{2,1,0:T(8,128)(2,1)} %bitcast.166), calls=%async_computation.6 | async-start | bytes 4194304 | tf_op jit(solution)/shard_map/all_to_all | solution.py:239
  324.1 60.5 %all-to-all-start.7 = ((bf16[16,64,2176]{2,1,0:T(8,128)(2,1)}), bf16[16,64,2176]{2,1,0:T(8,128)(2,1)}, u32[]{:S(2)}, u32[]{:S(2)}) async-start(bf16[16,64,2176]{2,1,0:T(8,128)(2,1)} %bitcast.149), calls=%async_computation.7 | async-start | bytes 8912896 | tf_op jit(solution)/shard_map/all_to_all | solution.py:239
  328.9 176.2 %reduce-scatter.3.cloned.1.call-start = ((), (), s32[]{:S(2)}) async-start(), calls=%async_computation.18 | async-start | bytes 15925248 | tf_op jit(solution)/shard_map/reduce_scatter | solution.py:441
  392.9 6.5 %collective-permute-start.2 = (bf16[64,2048]{1,0:T(8,128)(2,1)S(1)}, bf16[64,2048]{1,0:T(8,128)(2,1)S(1)}, u32[]{:S(2)}, u32[]{:S(2)}) collective-permute-start(bf16[64,2048]{1,0:T(8,128)(2,1)S(1)} %fusion.81), channel_id=1, source_target_pairs={{0,1},{1,0},{2,3},{3,2},{4,5},{5,4},{6,7},{7,6},{8,9},{9,8},{10,11... | collective-permute-start | bytes 786440 | tf_op jit(solution)/shard_map/ppermute | solution.py:65
  403.9 12.1 %all-to-all-start.8 = ((bf16[8,128,128]{2,1,0:T(8,128)(2,1)}), bf16[8,128,128]{2,1,0:T(8,128)(2,1)S(1)}, u32[]{:S(2)}, u32[]{:S(2)}) async-start(bf16[8,128,128]{2,1,0:T(8,128)(2,1)} %bitcast.145), calls=%async_computation.8 | async-start | bytes 524288 | tf_op jit(solution)/shard_map/all_to_all | solution.py:463
  416.0 30.0 %all-to-all-start.9 = ((bf16[16,64,1024]{2,1,0:T(8,128)(2,1)}), bf16[16,64,1024]{2,1,0:T(8,128)(2,1)}, u32[]{:S(2)}, u32[]{:S(2)}) async-start(bf16[16,64,1024]{2,1,0:T(8,128)(2,1)} %bitcast.159), calls=%async_computation.9 | async-start | bytes 4194304 | tf_op jit(solution)/shard_map/all_to_all | solution.py:239
  446.0 59.1 %all-to-all-start.10 = ((bf16[16,64,2048]{2,1,0:T(8,128)(2,1)}), bf16[16,64,2048]{2,1,0:T(8,128)(2,1)}, u32[]{:S(2)}, u32[]{:S(2)}) async-start(bf16[16,64,2048]{2,1,0:T(8,128)(2,1)} %bitcast.160), calls=%async_computation.10 | async-start | bytes 8388608 | tf_op jit(solution)/shard_map/all_to_all | solution.py:239
  451.0 99.7 %reduce-scatter.5.cloned.1.call-start = ((), (), s32[]{:S(2)}) async-start(), calls=%async_computation.19 | async-start | bytes 7077888 | tf_op jit(solution)/shard_map/reduce_scatter | solution.py:492
  456.9 27.2 %collective-permute-start.3 = (bf16[64,2048]{1,0:T(8,128)(2,1)S(1)}, bf16[64,2048]{1,0:T(8,128)(2,1)S(1)}, u32[]{:S(2)}, u32[]{:S(2)}) collective-permute-start(bf16[64,2048]{1,0:T(8,128)(2,1)S(1)} %fusion.64), channel_id=1, source_target_pairs={{0,1},{1,0},{2,3},{3,2},{4,5},{5,4},{6,7},{7,6},{8,9},{9,8},{10,11... | collective-permute-start | bytes 786440 | tf_op jit(solution)/shard_map/ppermute | solution.py:65
  505.2 34.9 %all-to-all-start.11 = ((bf16[8,32,3456]{2,1,0:T(8,128)(2,1)}), bf16[8,32,3456]{2,1,0:T(8,128)(2,1)S(1)}, u32[]{:S(2)}, u32[]{:S(2)}) async-start(bf16[8,32,3456]{2,1,0:T(8,128)(2,1)} %bitcast.167), calls=%async_computation.12 | async-start | bytes 3538944 | tf_op jit(solution)/shard_map/all_to_all | solution.py:502
  512.6 26.3 %collective-permute-start.4 = (f32[64,2048]{1,0:T(8,128)S(1)}, f32[64,2048]{1,0:T(8,128)S(1)}, u32[]{:S(2)}, u32[]{:S(2)}) collective-permute-start(f32[64,2048]{1,0:T(8,128)S(1)} %fusion.46), channel_id=1, source_target_pairs={{0,1},{1,0},{2,3},{3,2},{4,5},{5,4},{6,7},{7,6},{8,9},{9,8},{10,11... | collective-permute-start | bytes 1572872 | tf_op jit(solution)/shard_map/ppermute | solution.py:65
  551.9 22.1 %all-to-all-start.12 = ((bf16[8,32,1536]{2,1,0:T(8,128)(2,1)}), bf16[8,32,1536]{2,1,0:T(8,128)(2,1)S(1)}, u32[]{:S(2)}, u32[]{:S(2)}) async-start(bf16[8,32,1536]{2,1,0:T(8,128)(2,1)} %bitcast.172), calls=%async_computation.14 | async-start | bytes 1572864 | tf_op jit(solution)/shard_map/all_to_all | solution.py:505
  574.2 3.8 collective-permute-start.5
  (39 other events, 353.4 us)
Sparse Core Ops, SparseCore 0:
  25.9 51.6 all-gather.3
  79.9 31.8 all-gather.5
  125.5 74.0 all-gather.7
  384.8 82.0 reduce-scatter.2
  505.2 45.4 reduce-scatter.4

commit v4 on v3

--- a/solution.py
+++ b/solution.py
@@ -303,7 +303,7 @@
     slot_of = jnp.sum(
         jnp.where(chosen, position.reshape(rows, TOPK)[:, :, None] - (LANES - 1), 0), axis=1
     ) + (LANES - 1)
-    slot_cols = jnp.pad(mine(slot_of).astype(BF), ((0, 0), (0, LANES - experts)))
+    slot_cols = jnp.pad(slot_of.astype(BF), ((0, 0), (0, LANES - experts)))
     dy_own = mine(grad_out[0])
     x_own = mine(hidden_in[0])
 
@@ -349,13 +349,16 @@
 
     x_all = lax.all_gather(both_rings(hidden_in[0]), "ring", axis=1, tiled=True)
     x_all = x_all.reshape(length, width)
+    dy_slots = both_rings(jnp.concatenate([grad_out[0], slot_cols], 1))
 
     attn_blob = lax.all_to_all(attn_blob, SEQ, 0, 0, tiled=True).reshape(seqs * depth, -1)
     attn_cols = 3 * HD + LANES
     proj_rows = attn_blob[:, attn_cols:]
     attn_full = jnp.broadcast_to(attn_blob[None, :, :attn_cols], (dps, seqs * depth, attn_cols))
     attn_full = lax.all_to_all(attn_full, "dp", 0, 0, tiled=True).reshape(width, -1)
-    x_all, attn_full, proj_rows, ffn_blob = together(x_all, attn_full, proj_rows, ffn_blob)
+    x_all, attn_full, proj_rows, ffn_blob, dy_slots = together(
+        x_all, attn_full, proj_rows, ffn_blob, dy_slots
+    )
     proj_rows = lax.all_gather(proj_rows, "dp", axis=0, tiled=True)
     qkv_full = attn_full[:, : 3 * HD]
     misc_full = attn_full[:, 3 * HD :]
@@ -405,13 +408,11 @@
     probs_low = attn_probs.astype(BF)
     attn_head = mm(probs_low, value).astype(BF)
 
-    by_head, ffn_blob = together(attn_head.reshape(seqs, rows, HD), ffn_blob)
+    by_head, ffn_blob, dy_slots, proj_rows = together(
+        attn_head.reshape(seqs, rows, HD), ffn_blob, dy_slots, proj_rows
+    )
     by_head = lax.all_to_all(by_head, SEQ, 0, 0, tiled=True)
-    dy_slots = jnp.concatenate([dy_own, slot_cols], 1)
-    by_head, ffn_blob, dy_slots = together(by_head, ffn_blob, dy_slots)
-    dy_slots = plane_gather(dy_slots)
-    ffn_full = lax.all_gather(ffn_blob.reshape(seqs * depth, -1), "dp", axis=0, tiled=True)
-    w_up = ffn_full[:, : 2 * units]
+    dy_slots = lax.all_gather(dy_slots, "ring", axis=1, tiled=True)
     attn_flat = by_head.transpose(1, 0, 2).reshape(rows, heads * HD)
     attn_part = mm_nt(attn_flat, proj_rows)
     theirs = lax.dynamic_slice_in_dim(attn_part, (1 - me_tensor) * own, own, 0)
@@ -420,8 +421,12 @@
     scale_two = rms_scale(after_attn)
     norm_two = after_attn * scale_two
     normed_two = (norm_two * gain_ffn).astype(BF)
-    normed_sent, dy_slots = together(normed_two, dy_slots)
+    ffn_blob, dy_slots, normed_sent = together(
+        ffn_blob, dy_slots.reshape(length, width + LANES), normed_two
+    )
     h_all = plane_gather(normed_sent)
+    ffn_full = lax.all_gather(ffn_blob.reshape(seqs * depth, -1), "dp", axis=0, tiled=True)
+    w_up = ffn_full[:, : 2 * units]
 
     expert = me_seq.astype(jnp.int32).reshape(1)
     dgate_up, act_weighed, dots, router = feed_forward(

time: 593 us -> 589 us (level)
  blocking collectives: 20.9 us -> 0 us
  starting transfers between devices: 69.1 us -> 78.7 us
    all_gather x0 -> x1, waiting for transfers between devices: none -> 23 us  [body(): dy_slots = lax.all_gather(dy_slots, 'ring', axis=1, tiled=True)]
    all_to_all x2 -> x1, waiting for transfers between devices: 78.7 us -> 56.7 us  [plane_gather(): lax.all_to_all(copies, GRID, 0, 0, tiled=True).reshape(count * n, width)]
    all_to_all x1 -> x0, blocking collectives: 20.9 us -> none  [body(): lax.all_to_all(attn_blob, SEQ, 0, 0, tiled=True).reshape(seqs * depth, -1)]
    all_to_all x0 -> x1, waiting for transfers between devices: none -> 14.9 us  [body(): lax.all_to_all(attn_blob, SEQ, 0, 0, tiled=True).reshape(seqs * depth, -1)]
    all_to_all x4, waiting for transfers between devices: 68.4 us -> 56.8 us  [send_parts(): return lax.all_to_all(parts, GRID, 0, 0, tiled=True)]
    all_gather x1, waiting for transfers between devices: 0.01 us -> 8.68 us  [body(): lax.all_gather(ffn_blob.reshape(seqs * depth, -1), 'dp', axis=0, tiled=True)]
    reduce_scatter x1, waiting for transfers between devices: 10.6 us -> 3.59 us  [body(): lax.psum_scatter(attn_grad, 'dp', scatter_dimension=0, tiled=True)]
    unnamed x97 -> x107, local copies, waits for them, and re-layouts: 15.6 us -> 19.1 us
  transfers between devices with their start and end apart: 23 -> 25, of which waited for: 18 -> 19; matrix products, arithmetic and copies ran while one was open for 20% -> 21% of each run, Pallas kernels for 6% -> 6%
where the time goes in v4:
time: 589 us; the launch traced here: 582 us
  waiting for transfers between devices  287 us (49%)
  starting transfers between devices  78.7 us (13%)
  Pallas kernels  63.3 us (11%)
  matrix products  47.4 us (8%)
  local copies, waits for them, and re-layouts  45.6 us (8%)
  other arithmetic  44 us (7%)
  between operations  15.7 us (3%)
    ppermute x5, waiting for transfers between devices, swap(): return lax.ppermute(x, 'tensor', [(0, 1), (1, 0)])  69.8 us
    all_to_all x4, waiting for transfers between devices, send_parts(): return lax.all_to_all(parts, GRID, 0, 0, tiled=True)  56.8 us
    all_to_all x1, waiting for transfers between devices, plane_gather(): lax.all_to_all(copies, GRID, 0, 0, tiled=True).reshape(count * n, width)  56.7 us
    dot_general x14, matrix products, dot(): return lax.dot_general(a, b, (dims, ((), ())), preferred_element_type=F32)  47.4 us
    pallas_call x1, Pallas kernels, ffn_rest(): pl.pallas_call(ffn_rest_kernel, grid=(width // step,), in_specs=[pl.Block...  26.9 us
    pallas_call x1, Pallas kernels, feed_forward(): pl.pallas_call(functools.partial(feed_forward_kernel, capacity), grid_spe...  26.6 us
    all_gather x1, waiting for transfers between devices, body(): dy_slots = lax.all_gather(dy_slots, 'ring', axis=1, tiled=True)  23 us
    all_to_all x4, starting transfers between devices, send_parts(): return lax.all_to_all(parts, GRID, 0, 0, tiled=True)  21.2 us
  transfers between devices with their start and end apart: 25, of which 19 were waited for; matrix products, arithmetic and copies ran while one was open for 21% of the time, Pallas kernels for 6%

profile of v4, /device:TPU:4, one launch (start us, length us, event | category | flops | bytes accessed | tf_op | source)
XLA Modules:
  0.0 581.6 jit_solution(2824638629686349797)
XLA Ops:
  11.4 12.1 %collective-permute-done = bf16[128,2048]{1,0:T(8,128)(2,1)S(1)} collective-permute-done((bf16[128,2048]{1,0:T(8,128)(2,1)}, bf16[128,2048]{1,0:T(8,128)(2,1)S(1)}, u32[]{:S(2)}, u32[]{:S(2)}) %collective-permute-start) | collective-permute-done | bytes 524320 | tf_op jit(solution)/shard_map/ppermute | solution.py:61
  39.9 14.9 %all-to-all-done = bf16[8,32,1536]{2,1,0:T(8,128)(2,1)S(1)} async-done(((bf16[8,32,1536]{2,1,0:T(8,128)(2,1)}), bf16[8,32,1536]{2,1,0:T(8,128)(2,1)S(1)}, u32[]{:S(2)}, u32[]{:S(2)}) %all-to-all-start) | async-done | bytes 786464 | tf_op jit(solution)/shard_map/all_to_all | solution.py:354
  75.9 9.3 %all-to-all-done.1 = bf16[8,256,512]{2,1,0:T(8,128)(2,1)S(1)} async-done(((bf16[8,256,512]{2,1,0:T(8,128)(2,1)}), bf16[8,256,512]{2,1,0:T(8,128)(2,1)S(1)}, u32[]{:S(2)}, u32[]{:S(2)}) %all-to-all-start.1) | async-done | bytes 2097184 | tf_op jit(solution)/shard_map/all_to_all | solution.py:358
  86.3 7.0 %all-to-all-start.2 = ((bf16[8,32,3456]{2,1,0:T(8,128)(2,1)}), bf16[8,32,3456]{2,1,0:T(8,128)(2,1)}, u32[]{:S(2)}, u32[]{:S(2)}) async-start(bf16[8,32,3456]{2,1,0:T(8,128)(2,1)} %pad_dynamic-update-slice_fusion.1), calls=%async_computation.2 | async-start | bytes 3538944 | tf_op jit(solution)/shard_map/all_to_all | solution.py:365
  109.4 9.0 %all-to-all-done.2 = bf16[8,32,3456]{2,1,0:T(8,128)(2,1)} async-done(((bf16[8,32,3456]{2,1,0:T(8,128)(2,1)}), bf16[8,32,3456]{2,1,0:T(8,128)(2,1)}, u32[]{:S(2)}, u32[]{:S(2)}) %all-to-all-start.2) | async-done | bytes 1769504 | tf_op jit(solution)/shard_map/all_to_all | solution.py:365
  118.4 6.9 %all-to-all-start.3 = ((bf16[8,128,128]{2,1,0:T(8,128)(2,1)}), bf16[8,128,128]{2,1,0:T(8,128)(2,1)S(1)}, u32[]{:S(2)}, u32[]{:S(2)}) async-start(bf16[8,128,128]{2,1,0:T(8,128)(2,1)} %bitcast.31), calls=%async_computation.3 | async-start | bytes 524288 | tf_op jit(solution)/shard_map/all_to_all | solution.py:414
  125.3 9.1 %all-to-all-done.3 = bf16[8,128,128]{2,1,0:T(8,128)(2,1)S(1)} async-done(((bf16[8,128,128]{2,1,0:T(8,128)(2,1)}), bf16[8,128,128]{2,1,0:T(8,128)(2,1)S(1)}, u32[]{:S(2)}, u32[]{:S(2)}) %all-to-all-start.3) | async-done | bytes 262176 | tf_op jit(solution)/shard_map/all_to_all | solution.py:414
  140.1 7.2 %collective-permute-done.2 = bf16[64,2048]{1,0:T(8,128)(2,1)S(1)} collective-permute-done((bf16[64,2048]{1,0:T(8,128)(2,1)S(1)}, bf16[64,2048]{1,0:T(8,128)(2,1)S(1)}, u32[]{:S(2)}, u32[]{:S(2)}) %collective-permute-start.2) | collective-permute-done | bytes 262176 | tf_op jit(solution)/shard_map/ppermute | solution.py:65
  148.8 23.0 %all-gather.9.cloned.1.call-done = bf16[2,512,2176]{2,1,0:T(8,128)(2,1)} async-done(((bf16[2,128,2176]{2,1,0:T(8,128)(2,1)}), bf16[2,512,2176]{2,1,0:T(8,128)(2,1)}) %all-gather.9.cloned.1.call-update) | async-done | bytes 4456464 | tf_op jit(solution)/shard_map/all_gather | solution.py:415
  181.5 56.7 %all-to-all-done.4 = bf16[16,64,2048]{2,1,0:T(8,128)(2,1)} async-done(((bf16[16,64,2048]{2,1,0:T(8,128)(2,1)}), bf16[16,64,2048]{2,1,0:T(8,128)(2,1)}, u32[]{:S(2)}, u32[]{:S(2)}) %all-to-all-start.4) | async-done | bytes 4194336 | tf_op jit(solution)/shard_map/all_to_all | solution.py:233
  238.2 8.7 %all-gather.11.cloned.1.call-done.up_ref.down_ref = bf16[2048,3456]{1,0:T(8,128)(2,1)} async-done(((bf16[256,3456]{1,0:T(8,128)(2,1)}), bf16[2048,3456]{1,0:T(8,128)(2,1)}) %all-gather.11.cloned.1.call-update) | async-done | bytes 14155792 | tf_op jit(solution)/shard_map/all_gather | solution.py:428
  246.9 26.6 %shard_map.255 = (bf16[1024,2304]{1,0:T(8,128)(2,1)}, bf16[1024,1152]{1,0:T(8,128)(2,1)}, f32[1024,128]{1,0:T(8,128)}, f32[1024,128]{1,0:T(8,128)}) custom-call(s32[1]{0:T(128)} %bitcast.33.expert_ref, bf16[1024,2048]{1,0:T(8,128)(2,1)} %bitcast.35.h_ref, bf16[1024,2176]{1,0:T(8,128)(2,1)} %bitcast.155, ...), custom_call_target="tpu_custom_call" | custom-call | tf_op jit(solution)/shard_map/pallas_call | solution.py:137
  273.5 6.7 %fusion.15 = bf16[1024,1024]{1,0:T(8,128)(2,1)} fusion(bf16[1024,1152]{1,0:T(8,128)(2,1)} %get-tuple-element.66.act_ref, bf16[2048,3456]{1,0:T(8,128)(2,1)} %all-gather.11.cloned.1.call-done.up_ref.down_ref), kind=kOutput, calls=%fused_computation.26 | convolution fusion | flops 2416967680 | bytes 6815744 | tf_op jit(solution)/shard_map/dot_general | solution.py:32
  280.2 7.0 %all-to-all-start.5 = ((bf16[16,64,1024]{2,1,0:T(8,128)(2,1)}), bf16[16,64,1024]{2,1,0:T(8,128)(2,1)}, u32[]{:S(2)}, u32[]{:S(2)}) async-start(bf16[16,64,1024]{2,1,0:T(8,128)(2,1)} %bitcast.176), calls=%async_computation.5 | async-start | bytes 4194304 | tf_op jit(solution)/shard_map/all_to_all | solution.py:239
  288.3 13.9 %fusion.8 = bf16[1024,2048]{1,0:T(8,128)(2,1)S(1)} fusion(bf16[1024,2304]{1,0:T(8,128)(2,1)} %get-tuple-element.65.middle_ref, bf16[2048,3456]{1,0:T(8,128)(2,1)} %all-gather.11.cloned.1.call-done.up_ref.down_ref), kind=kOutput, calls=%fused_computation.20 | convolution fusion | flops 9665773568 | bytes 18350080 | tf_op jit(solution)/shard_map/dot_general | solution.py:32
  304.7 14.2 %all-to-all-done.5 = bf16[16,64,1024]{2,1,0:T(8,128)(2,1)} async-done(((bf16[16,64,1024]{2,1,0:T(8,128)(2,1)}), bf16[16,64,1024]{2,1,0:T(8,128)(2,1)}, u32[]{:S(2)}, u32[]{:S(2)}) %all-to-all-start.5) | async-done | bytes 2097184 | tf_op jit(solution)/shard_map/all_to_all | solution.py:239
  323.7 26.9 %shard_map.256 = (bf16[2048,3456]{1,0:T(8,128)(2,1)}, bf16[1024,2048]{1,0:T(8,128)(2,1)}) custom-call(bf16[1024,2048]{1,0:T(8,128)(2,1)} %bitcast.35.h_ref, bf16[1024,2176]{1,0:T(8,128)(2,1)} %bitcast.156, bf16[1024,2304]{1,0:T(8,128)(2,1)} %get-tuple-element.65.middle_ref, bf16[1024,1152]{1,0:T(8,128)(2,1)} %get-tuple-element.66.act_ref, ...), custom_call_target="tpu_custom_call" | custom-call | tf_op jit(solution)/shard_map/pallas_call | solution.py:178
  350.6 33.1 %all-to-all-done.6 = bf16[16,64,2176]{2,1,0:T(8,128)(2,1)} async-done(((bf16[16,64,2176]{2,1,0:T(8,128)(2,1)}), bf16[16,64,2176]{2,1,0:T(8,128)(2,1)}, u32[]{:S(2)}, u32[]{:S(2)}) %all-to-all-start.6) | async-done | bytes 4456480 | tf_op jit(solution)/shard_map/all_to_all | solution.py:239
  440.2 9.6 %all-to-all-done.8 = bf16[16,64,1024]{2,1,0:T(8,128)(2,1)} async-done(((bf16[16,64,1024]{2,1,0:T(8,128)(2,1)}), bf16[16,64,1024]{2,1,0:T(8,128)(2,1)}, u32[]{:S(2)}, u32[]{:S(2)}) %all-to-all-start.8) | async-done | bytes 2097184 | tf_op jit(solution)/shard_map/all_to_all | solution.py:239
  464.3 9.8 %shard_map.257 = bf16[2048,1536]{1,0:T(8,128)(2,1)} custom-call(bf16[1024,2048]{1,0:T(8,128)(2,1)} %copy-done, bf16[1024,384]{1,0:T(8,128)(2,1)} %copy-done.4, f32[128,2048]{1,0:T(8,128)} %select_maximum_fusion.small_ref, bf16[128,2048]{1,0:T(8,128)(2,1)} %pad_maximum_fusion.4.dx_ref, bf16[128,1024]{1,0:T(8,128)(2,1)} %copy_bitcast_fusion.2.heads_ref), custom_call_target="tpu_custom_call" | custom-call | tf_op jit(solution)/shard_map/pallas_call | solution.py:213
  474.1 30.7 %collective-permute-done.4 = bf16[64,2048]{1,0:T(8,128)(2,1)S(1)} collective-permute-done((bf16[64,2048]{1,0:T(8,128)(2,1)S(1)}, bf16[64,2048]{1,0:T(8,128)(2,1)S(1)}, u32[]{:S(2)}, u32[]{:S(2)}) %collective-permute-start.4) | collective-permute-done | bytes 262176 | tf_op jit(solution)/shard_map/ppermute | solution.py:65
  514.7 26.1 %collective-permute-done.5 = f32[64,2048]{1,0:T(8,128)S(1)} collective-permute-done((f32[64,2048]{1,0:T(8,128)S(1)}, f32[64,2048]{1,0:T(8,128)S(1)}, u32[]{:S(2)}, u32[]{:S(2)}) %collective-permute-start.5) | collective-permute-done | bytes 524320 | tf_op jit(solution)/shard_map/ppermute | solution.py:65
  546.8 6.7 %all-to-all-start.11 = ((bf16[8,32,1536]{2,1,0:T(8,128)(2,1)}), bf16[8,32,1536]{2,1,0:T(8,128)(2,1)S(1)}, u32[]{:S(2)}, u32[]{:S(2)}) async-start(bf16[8,32,1536]{2,1,0:T(8,128)(2,1)} %bitcast.182), calls=%async_computation.13 | async-start | bytes 1572864 | tf_op jit(solution)/shard_map/all_to_all | solution.py:510
  560.6 8.3 %all-to-all-done.11 = bf16[8,32,1536]{2,1,0:T(8,128)(2,1)S(1)} async-done(((bf16[8,32,1536]{2,1,0:T(8,128)(2,1)}), bf16[8,32,1536]{2,1,0:T(8,128)(2,1)S(1)}, u32[]{:S(2)}, u32[]{:S(2)}) %all-to-all-start.11) | async-done | bytes 786464 | tf_op jit(solution)/shard_map/all_to_all | solution.py:510
  (278 shorter events, 182.6 us)
Async XLA Ops:
  7.3 78.0 %all-gather.5.cloned.1.call-start = ((), (), s32[]{:S(2)}) async-start(), calls=%async_computation.14 | async-start | bytes 5242880 | tf_op jit(solution)/shard_map/all_gather | solution.py:350
  7.3 16.3 %collective-permute-start = (bf16[128,2048]{1,0:T(8,128)(2,1)}, bf16[128,2048]{1,0:T(8,128)(2,1)S(1)}, u32[]{:S(2)}, u32[]{:S(2)}) collective-permute-start(bf16[128,2048]{1,0:T(8,128)(2,1)} %bitcast.171), channel_id=1, source_target_pairs={{0,9},{1,8},{2,11},{3,10},{4,13},{5,12},{6,15},{7,14},{8,1},{9,0},... | collective-permute-start | bytes 1572872 | tf_op jit(solution)/shard_map/ppermute | solution.py:61
  27.8 43.8 %collective-permute-start.1 = (bf16[128,2176]{1,0:T(8,128)(2,1)}, bf16[128,2176]{1,0:T(8,128)(2,1)}, u32[]{:S(2)}, u32[]{:S(2)}) collective-permute-start(bf16[128,2176]{1,0:T(8,128)(2,1)} %fusion.43), channel_id=1, source_target_pairs={{0,9},{1,8},{2,11},{3,10},{4,13},{5,12},{6,15},{7,14},{8,1},{9,0},... | collective-permute-start | bytes 1671176 | tf_op jit(solution)/shard_map/ppermute | solution.py:61
  32.8 21.9 %all-to-all-start = ((bf16[8,32,1536]{2,1,0:T(8,128)(2,1)}), bf16[8,32,1536]{2,1,0:T(8,128)(2,1)S(1)}, u32[]{:S(2)}, u32[]{:S(2)}) async-start(bf16[8,32,1536]{2,1,0:T(8,128)(2,1)} %concatenate.77), calls=%async_computation | async-start | bytes 1572864 | tf_op jit(solution)/shard_map/all_to_all | solution.py:354
  56.4 28.9 %all-to-all-start.1 = ((bf16[8,256,512]{2,1,0:T(8,128)(2,1)}), bf16[8,256,512]{2,1,0:T(8,128)(2,1)S(1)}, u32[]{:S(2)}, u32[]{:S(2)}) async-start(bf16[8,256,512]{2,1,0:T(8,128)(2,1)} %broadcast_in_dim.115), calls=%async_computation.1 | async-start | bytes 4194304 | tf_op jit(solution)/shard_map/all_to_all | solution.py:358
  61.2 57.2 %all-gather.7.cloned.1.call-start = ((), (), s32[]{:S(2)}) async-start(), calls=%async_computation.15 | async-start | bytes 4718592 | tf_op jit(solution)/shard_map/all_gather | solution.py:362
  86.3 32.1 %all-to-all-start.2 = ((bf16[8,32,3456]{2,1,0:T(8,128)(2,1)}), bf16[8,32,3456]{2,1,0:T(8,128)(2,1)}, u32[]{:S(2)}, u32[]{:S(2)}) async-start(bf16[8,32,3456]{2,1,0:T(8,128)(2,1)} %pad_dynamic-update-slice_fusion.1), calls=%async_computation.2 | async-start | bytes 3538944 | tf_op jit(solution)/shard_map/all_to_all | solution.py:365
  93.2 78.6 %all-gather.9.cloned.1.call-start = ((), (), s32[]{:S(2)}) async-start(), calls=%async_computation.16 | async-start | bytes 5570560 | tf_op jit(solution)/shard_map/all_gather | solution.py:415
  118.4 16.1 %all-to-all-start.3 = ((bf16[8,128,128]{2,1,0:T(8,128)(2,1)}), bf16[8,128,128]{2,1,0:T(8,128)(2,1)S(1)}, u32[]{:S(2)}, u32[]{:S(2)}) async-start(bf16[8,128,128]{2,1,0:T(8,128)(2,1)} %bitcast.31), calls=%async_computation.3 | async-start | bytes 524288 | tf_op jit(solution)/shard_map/all_to_all | solution.py:414
  125.3 121.6 %all-gather.11.cloned.1.call-start = ((), (), s32[]{:S(2)}) async-start(), calls=%async_computation.17 | async-start | bytes 15925248 | tf_op jit(solution)/shard_map/all_gather | solution.py:428
  139.3 8.0 %collective-permute-start.2 = (bf16[64,2048]{1,0:T(8,128)(2,1)S(1)}, bf16[64,2048]{1,0:T(8,128)(2,1)S(1)}, u32[]{:S(2)}, u32[]{:S(2)}) collective-permute-start(bf16[64,2048]{1,0:T(8,128)(2,1)S(1)} %dynamic-slice_convert_fusion), channel_id=1, source_target_pairs={{0,1},{1,0},{2,3},{3,2},{4,5},{5,4},{6,7},{7,6},{8,9},{9,8},{10,11... | collective-permute-start | bytes 786440 | tf_op jit(solution)/shard_map/ppermute | solution.py:65
  174.3 63.8 %all-to-all-start.4 = ((bf16[16,64,2048]{2,1,0:T(8,128)(2,1)}), bf16[16,64,2048]{2,1,0:T(8,128)(2,1)}, u32[]{:S(2)}, u32[]{:S(2)}) async-start(bf16[16,64,2048]{2,1,0:T(8,128)(2,1)} %broadcast_in_dim.120), calls=%async_computation.4 | async-start | bytes 8388608 | tf_op jit(solution)/shard_map/all_to_all | solution.py:233
  280.2 38.7 %all-to-all-start.5 = ((bf16[16,64,1024]{2,1,0:T(8,128)(2,1)}), bf16[16,64,1024]{2,1,0:T(8,128)(2,1)}, u32[]{:S(2)}, u32[]{:S(2)}) async-start(bf16[16,64,1024]{2,1,0:T(8,128)(2,1)} %bitcast.176), calls=%async_computation.5 | async-start | bytes 4194304 | tf_op jit(solution)/shard_map/all_to_all | solution.py:239
  318.8 64.8 %all-to-all-start.6 = ((bf16[16,64,2176]{2,1,0:T(8,128)(2,1)}), bf16[16,64,2176]{2,1,0:T(8,128)(2,1)}, u32[]{:S(2)}, u32[]{:S(2)}) async-start(bf16[16,64,2176]{2,1,0:T(8,128)(2,1)} %bitcast.157), calls=%async_computation.6 | async-start | bytes 8912896 | tf_op jit(solution)/shard_map/all_to_all | solution.py:239
  323.6 182.1 %reduce-scatter.3.cloned.1.call-start = ((), (), s32[]{:S(2)}) async-start(), calls=%async_computation.18 | async-start | bytes 15925248 | tf_op jit(solution)/shard_map/reduce_scatter | solution.py:446
  392.9 6.4 %collective-permute-start.3 = (bf16[64,2048]{1,0:T(8,128)(2,1)S(1)}, bf16[64,2048]{1,0:T(8,128)(2,1)S(1)}, u32[]{:S(2)}, u32[]{:S(2)}) collective-permute-start(bf16[64,2048]{1,0:T(8,128)(2,1)S(1)} %fusion.81), channel_id=1, source_target_pairs={{0,1},{1,0},{2,3},{3,2},{4,5},{5,4},{6,7},{7,6},{8,9},{9,8},{10,11... | collective-permute-start | bytes 786440 | tf_op jit(solution)/shard_map/ppermute | solution.py:65
  403.8 12.9 %all-to-all-start.7 = ((bf16[8,128,128]{2,1,0:T(8,128)(2,1)}), bf16[8,128,128]{2,1,0:T(8,128)(2,1)S(1)}, u32[]{:S(2)}, u32[]{:S(2)}) async-start(bf16[8,128,128]{2,1,0:T(8,128)(2,1)} %bitcast.151), calls=%async_computation.7 | async-start | bytes 524288 | tf_op jit(solution)/shard_map/all_to_all | solution.py:468
  416.7 33.1 %all-to-all-start.8 = ((bf16[16,64,1024]{2,1,0:T(8,128)(2,1)}), bf16[16,64,1024]{2,1,0:T(8,128)(2,1)}, u32[]{:S(2)}, u32[]{:S(2)}) async-start(bf16[16,64,1024]{2,1,0:T(8,128)(2,1)} %bitcast.167), calls=%async_computation.8 | async-start | bytes 4194304 | tf_op jit(solution)/shard_map/all_to_all | solution.py:239
  449.8 55.9 %all-to-all-start.9 = ((bf16[16,64,2048]{2,1,0:T(8,128)(2,1)}), bf16[16,64,2048]{2,1,0:T(8,128)(2,1)}, u32[]{:S(2)}, u32[]{:S(2)}) async-start(bf16[16,64,2048]{2,1,0:T(8,128)(2,1)} %bitcast.170), calls=%async_computation.9 | async-start | bytes 8388608 | tf_op jit(solution)/shard_map/all_to_all | solution.py:239
  454.8 90.8 %reduce-scatter.5.cloned.1.call-start = ((), (), s32[]{:S(2)}) async-start(), calls=%async_computation.19 | async-start | bytes 7077888 | tf_op jit(solution)/shard_map/reduce_scatter | solution.py:497
  460.7 44.1 %collective-permute-start.4 = (bf16[64,2048]{1,0:T(8,128)(2,1)S(1)}, bf16[64,2048]{1,0:T(8,128)(2,1)S(1)}, u32[]{:S(2)}, u32[]{:S(2)}) collective-permute-start(bf16[64,2048]{1,0:T(8,128)(2,1)S(1)} %fusion.65), channel_id=1, source_target_pairs={{0,1},{1,0},{2,3},{3,2},{4,5},{5,4},{6,7},{7,6},{8,9},{9,8},{10,11... | collective-permute-start | bytes 786440 | tf_op jit(solution)/shard_map/ppermute | solution.py:65
  505.8 36.2 %all-to-all-start.10 = ((bf16[8,32,3456]{2,1,0:T(8,128)(2,1)}), bf16[8,32,3456]{2,1,0:T(8,128)(2,1)S(1)}, u32[]{:S(2)}, u32[]{:S(2)}) async-start(bf16[8,32,3456]{2,1,0:T(8,128)(2,1)} %bitcast.177), calls=%async_computation.11 | async-start | bytes 3538944 | tf_op jit(solution)/shard_map/all_to_all | solution.py:507
  514.4 26.4 %collective-permute-start.5 = (f32[64,2048]{1,0:T(8,128)S(1)}, f32[64,2048]{1,0:T(8,128)S(1)}, u32[]{:S(2)}, u32[]{:S(2)}) collective-permute-start(f32[64,2048]{1,0:T(8,128)S(1)} %fusion.47), channel_id=1, source_target_pairs={{0,1},{1,0},{2,3},{3,2},{4,5},{5,4},{6,7},{7,6},{8,9},{9,8},{10,11... | collective-permute-start | bytes 1572872 | tf_op jit(solution)/shard_map/ppermute | solution.py:65
  546.8 22.1 %all-to-all-start.11 = ((bf16[8,32,1536]{2,1,0:T(8,128)(2,1)}), bf16[8,32,1536]{2,1,0:T(8,128)(2,1)S(1)}, u32[]{:S(2)}, u32[]{:S(2)}) async-start(bf16[8,32,1536]{2,1,0:T(8,128)(2,1)} %bitcast.182), calls=%async_computation.13 | async-start | bytes 1572864 | tf_op jit(solution)/shard_map/all_to_all | solution.py:510
  (46 other events, 448.6 us)
Sparse Core Ops, SparseCore 0:
  25.9 56.2 all-gather.4
  85.4 32.9 all-gather.6
  120.0 51.7 all-gather.8
  173.3 73.4 all-gather.10
  383.8 76.2 reduce-scatter.2
  505.8 39.6 reduce-scatter.4
